TPU v7x, 128 devices: a whole 4x4x4 slice. The times are simulated.
128 devices in a mesh: seq: 32 (over y, x, core), head: 4 (over z).
Axes of the slice: x: 4, y: 4, z: 4, core: 2. Of those that a mesh axis runs over, the one named last changes fastest.
Arguments:
- query_matrix_rows: bfloat16 [8192, 2048], P('seq', 'head'), may hold values from -6 to 6
- key_matrix_rows: bfloat16 [8192, 2048], P('seq', 'head'), may hold values from -6 to 6
- value_matrix_rows: bfloat16 [8192, 4096], P('seq', 'head'), may hold values from -6 to 6
- write_strength: float32 [32, 8192], P('head', 'seq'), may hold values from 0 to 1
- forget_gate_code: int32 [32, 8192], P('head', 'seq'), may hold values from 0 to 52
- value_to_key_head: int32 [32], P('head'), may hold values from 0 to 15, as said below
- output_norm_gain: float32 [128], replicated, may hold values from 0.1 to 1.9
- output_weight: bfloat16 [4096, 2048], P('head'), may hold values from -0.09375 to 0.09375
- adapter_lowering: float32 [16, 4096], P(None, 'head'), may hold values from -0.09375 to 0.09375
- adapter_raising: float32 [16, 2048], replicated, may hold values from -1.5 to 1.5
- output_gradient: bfloat16 [8192, 2048], P('seq'), may hold values from -6 to 6
Outputs:
- grad_query: float32 [8192, 2048], P('seq', 'head')
- grad_key: float32 [8192, 2048], P('seq', 'head')
- grad_value: float32 [8192, 4096], P('seq', 'head')
- grad_rate: float32 [32, 8192], P('head', 'seq')
- grad_down: float32 [16, 4096], P(None, 'head')
- raising_gradient: float32 [16, 2048], replicated
Inputs may be any that keep to these rules, and one draw needn't show every extreme that they name: `value_to_key_head`: value heads g * 8 to g * 8 + 7 read only key heads g * 4 to g * 4 + 3, each of these exactly 8 // 4 times.
All inputs are finite; a program needn't handle non-finite values.
Results may differ from a plain program's by a relative error of at most 0.00035.
Values sent between devices are 32-bit elements; how exact they have to be, the bound alone decides.
A program may use at most 192 MiB of HBM per device.

v0:
```python
import jax
import jax.numpy as jnp
from jax import lax
from jax.sharding import PartitionSpec as P

DK = 128
VALUE_HEAD_SIZE = 128
BLOCK = 64


adapter_scale = 2.0


def prefix(value, axis, join, neutral, backward):
    count, mine = (lax.axis_size(axis), lax.axis_index(axis))
    pieces = jax.tree.map(lambda part: lax.all_gather(part, axis), value)
    if backward:
        pieces = jax.tree.map(lambda part: part[::-1], pieces)
        mine = count - 1 - mine
    subtotal = jax.tree.map(
        lambda part, zero: jnp.full_like(part, 0) + jnp.asarray(zero, part.dtype), value, neutral
    )

    def turn(position, subtotal):
        longer = join(subtotal, jax.tree.map(lambda part: part[position], pieces))
        return jax.tree.map(lambda new, old: jnp.where(position < mine, new, old), longer, subtotal)

    return lax.fori_loop(0, count - 1, turn, subtotal)


def unit_rows(array):
    return array * lax.rsqrt(jnp.sum(array * array, axis=-1, keepdims=True) + 1e-06)


def block_step(state, block_items):
    query_block, key_block, value_block, rate_block, log_block = block_items
    finest_precision = lax.Precision.HIGHEST
    cumlog = jnp.cumsum(log_block, axis=-1)
    width = log_block.shape[-1]
    row_index = jnp.arange(width)[:, None]
    col_index = jnp.arange(width)[None, :]
    gap_log = cumlog[..., :, None] - cumlog[..., None, :]
    decays = jnp.exp(jnp.where(row_index >= col_index, gap_log, 0.0))
    key_dots = jnp.einsum("hcd,hed->hce", key_block, key_block, precision=finest_precision)
    strict_part = jnp.where(
        row_index > col_index, decays * key_dots * rate_block[..., None, :], 0.0
    )
    identity = jnp.eye(width, dtype=strict_part.dtype)
    start_decay = jnp.exp(cumlog)[..., None]
    targets = value_block - start_decay * jnp.einsum(
        "hcd,hdw->hcw", key_block, state, precision=finest_precision
    )
    deltas = lax.linalg.triangular_solve(
        identity + strict_part, targets, left_side=True, lower=True, unit_diagonal=True
    )
    end_log = cumlog[..., -1]
    weight = (jnp.exp(end_log[..., None] - cumlog) * rate_block)[..., None]
    new_state = jnp.exp(end_log)[..., None, None] * state + jnp.einsum(
        "hcd,hcw->hdw", key_block * weight, deltas, precision=finest_precision
    )
    if query_block is None:
        return (new_state, None)
    query_dots = jnp.einsum("hcd,hed->hce", query_block, key_block, precision=finest_precision)
    mixing = jnp.where(row_index >= col_index, decays * query_dots * rate_block[..., None, :], 0.0)
    result = start_decay * jnp.einsum(
        "hcd,hdw->hcw", query_block, state, precision=finest_precision
    )
    result = result + jnp.einsum("hce,hew->hcw", mixing, deltas, precision=finest_precision)
    return (new_state, result)


def run_blocks(query_heads, key_heads, value_heads, rate_heads, log_heads, state):
    head_count = rate_heads.shape[0]
    length = rate_heads.shape[1]
    block_count = length // BLOCK

    def to_blocks(array):
        return jnp.moveaxis(array.reshape((head_count, block_count, BLOCK) + array.shape[2:]), 1, 0)

    query_part = None if query_heads is None else to_blocks(query_heads)
    block_items = (
        query_part,
        to_blocks(key_heads),
        to_blocks(value_heads),
        to_blocks(rate_heads),
        to_blocks(log_heads),
    )
    state, results = lax.scan(block_step, state, block_items)
    if results is not None:
        results = jnp.moveaxis(results, 0, 1).reshape(head_count, length, results.shape[-1])
    return (state, results)


def compose(first_part, second_part):
    finest_precision = lax.Precision.HIGHEST
    matrix = jnp.einsum("hij,hjk->hik", second_part[0], first_part[0], precision=finest_precision)
    offset = (
        jnp.einsum("hij,hjk->hik", second_part[0], first_part[1], precision=finest_precision)
        + second_part[1]
    )
    return (matrix, offset)


def body(
    query_matrix_rows,
    key_matrix_rows,
    value_matrix_rows,
    write_strength,
    forget_gate_code,
    value_to_key_head,
    output_norm_gain,
    output_weight,
    adapter_lowering,
    adapter_raising,
    output_gradient,
):
    finest_precision = lax.Precision.HIGHEST
    local_heads = write_strength.shape[0]
    tokens = write_strength.shape[1]
    local_keys = query_matrix_rows.shape[1] // DK
    key_select = (
        (value_to_key_head % local_keys)[:, None]
        == jnp.arange(local_keys, dtype=jnp.int32)[None, :]
    ).astype(jnp.float32)
    log_gate = jnp.log1p(-forget_gate_code.astype(jnp.float32) * 2.0 ** (-20))
    query_float = query_matrix_rows.astype(jnp.float32)
    key_float = key_matrix_rows.astype(jnp.float32)
    value_float = value_matrix_rows.astype(jnp.float32)

    def spread(rows):
        shaped = unit_rows(rows.reshape(tokens, local_keys, DK))
        return jnp.einsum("tgd,hg->htd", shaped, key_select, precision=finest_precision)

    def norm_rows(outputs):
        return (
            outputs
            * lax.rsqrt(jnp.mean(outputs * outputs, axis=-1, keepdims=True) + 1e-06)
            * output_norm_gain
        )

    def forward(query_in, key_in, value_in, rate_in, state_in):
        query_heads = spread(query_in) * DK ** (-0.5)
        key_heads = spread(key_in)
        value_heads = jnp.moveaxis(value_in.reshape(tokens, local_heads, VALUE_HEAD_SIZE), 1, 0)
        state_out, outputs = run_blocks(
            query_heads, key_heads, value_heads, rate_in, log_gate, state_in
        )
        return ((norm_rows(outputs), state_out), outputs)

    identity = jnp.broadcast_to(jnp.eye(DK, dtype=jnp.float32), (local_heads, DK, DK))
    zero_state = jnp.zeros((local_heads, DK, VALUE_HEAD_SIZE), jnp.float32)
    key_spread = spread(key_float)
    query_spread = spread(query_float) * DK ** (-0.5)
    summary_values = jnp.concatenate(
        [
            jnp.zeros((local_heads, tokens, DK), jnp.float32),
            jnp.moveaxis(value_float.reshape(tokens, local_heads, VALUE_HEAD_SIZE), 1, 0),
        ],
        axis=-1,
    )
    summary, unused = run_blocks(
        None,
        key_spread,
        summary_values,
        write_strength,
        log_gate,
        jnp.concatenate([identity, zero_state], axis=-1),
    )
    transfer = summary[..., :DK]
    offset = summary[..., DK:]
    state_in = prefix((transfer, offset), "seq", compose, (identity, zero_state), False)[1]
    (normalized_output, state_out), pullback, outputs = jax.vjp(
        forward, query_float, key_float, value_float, write_strength, state_in, has_aux=True
    )
    normalized_rows = jnp.moveaxis(normalized_output, 0, 1).reshape(
        tokens, local_heads * VALUE_HEAD_SIZE
    )
    gradient_single = output_gradient.astype(jnp.float32)
    projected_output = lax.dot_general(
        output_gradient, output_weight, (((1,), (1,)), ((), ())), preferred_element_type=jnp.float32
    )
    gradient_lowrank = jnp.dot(gradient_single, adapter_raising.T, precision=finest_precision)
    gradient_normalized = projected_output + adapter_scale * jnp.dot(
        gradient_lowrank, adapter_lowering, precision=finest_precision
    )
    grad_heads = jnp.moveaxis(
        gradient_normalized.reshape(tokens, local_heads, VALUE_HEAD_SIZE), 1, 0
    )
    lowering_piece = adapter_scale * jnp.dot(
        gradient_lowrank.T, normalized_rows, precision=finest_precision
    )
    lowrank_piece = jnp.dot(normalized_rows, adapter_lowering.T, precision=finest_precision)
    lowrank_total = lax.psum(lowrank_piece, "head")
    raising_piece = adapter_scale * jnp.dot(
        lowrank_total.T, gradient_single, precision=finest_precision
    )
    grad_down, raising_gradient = lax.psum((lowering_piece, raising_piece), "seq")
    grad_outputs = jax.vjp(norm_rows, outputs)[1](grad_heads)[0]
    zero_values = jnp.zeros((local_heads, tokens, VALUE_HEAD_SIZE), jnp.float32)

    def state_reading(state_value):
        return run_blocks(
            query_spread, key_spread, zero_values, write_strength, log_gate, state_value
        )[1]

    local_adjoint = jax.vjp(state_reading, zero_state)[1](grad_outputs)[0]
    transposed = jnp.swapaxes(transfer, 1, 2)
    state_grad = prefix((transposed, local_adjoint), "seq", compose, (identity, zero_state), True)[
        1
    ]
    grad_query, grad_key, grad_value, grad_rate, unused_state = pullback((grad_heads, state_grad))
    return (grad_query, grad_key, grad_value, grad_rate, grad_down, raising_gradient)


def solution(mesh):
    placed = (
        P("seq", "head"),
        P("seq", "head"),
        P("seq", "head"),
        P("head", "seq"),
        P("head", "seq"),
        P("head"),
        P(),
        P("head", None),
        P(None, "head"),
        P(),
        P("seq", None),
    )
    return jax.shard_map(
        body,
        mesh=mesh,
        in_specs=placed,
        out_specs=(
            P("seq", "head"),
            P("seq", "head"),
            P("seq", "head"),
            P("head", "seq"),
            P(None, "head"),
            P(),
        ),
        check_vma=False,
    )
```

profile of v0, /device:TPU:1, one launch (start us, length us, event | category | flops | bytes accessed | tf_op | source)
XLA Modules:
  0.0 1490.6 jit_solution(16432885771661335509)
XLA Ops:
  16.5 183.8 %while.143 = (s32[]{:T(128)}, f32[8,128,256]{2,1,0:T(8,128)S(1)}, f32[4,8,64]{2,1,0:T(8,128)S(1)}, f32[4,8,64,128]{3,2,1,0:T(8,128)S(1)}, f32[4,8,64]{2,1,0:T(8,...) while((s32[]{:T(128)}, f32[8,128,256]{2,1,0:T(8,128)S(1)}, f32[4,8,64]{2,1,0:T(8,128)S(1)}, ...), condition=%wide.region_3.4_spmd, body=%wide.region_1.3_spmd.sunk | while | flops 554824256 | bytes 6992137 | solution.py:88
  18.4 40.0 %custom-call.39 = f32[8,1,64,64]{2,3,1,0:T(8,128)S(1)} custom-call(f32[8,1,64,64]{3,2,1,0:T(8,128)} %fusion.339), custom_call_target="InvertDiagBlocksLowerTriangular" | custom-call | tf_op jit(solution)/shard_map/while/body/eval_jaxpr/triangular_solve | solution.py:53
  64.3 40.0 %custom-call.39 = f32[8,1,64,64]{2,3,1,0:T(8,128)S(1)} custom-call(f32[8,1,64,64]{3,2,1,0:T(8,128)} %fusion.339), custom_call_target="InvertDiagBlocksLowerTriangular" | custom-call | tf_op jit(solution)/shard_map/while/body/eval_jaxpr/triangular_solve | solution.py:53
  110.3 40.0 %custom-call.39 = f32[8,1,64,64]{2,3,1,0:T(8,128)S(1)} custom-call(f32[8,1,64,64]{3,2,1,0:T(8,128)} %fusion.339), custom_call_target="InvertDiagBlocksLowerTriangular" | custom-call | tf_op jit(solution)/shard_map/while/body/eval_jaxpr/triangular_solve | solution.py:53
  156.2 40.0 %custom-call.39 = f32[8,1,64,64]{2,3,1,0:T(8,128)S(1)} custom-call(f32[8,1,64,64]{3,2,1,0:T(8,128)} %fusion.339), custom_call_target="InvertDiagBlocksLowerTriangular" | custom-call | tf_op jit(solution)/shard_map/while/body/eval_jaxpr/triangular_solve | solution.py:53
  218.5 22.0 %while.145 = (s32[]{:T(128)}, f32[4,8,64,1]{2,1,3,0:T(8,128)}, f32[4,8,64,64]{3,2,1,0:T(8,128)}, f32[4,8,1,1]{1,3,2,0:T(1,128)S(1)}, f32[4,8,64,128]{3,2,1,0:T(8...) while((s32[]{:T(128)}, f32[4,8,64,1]{2,1,3,0:T(8,128)}, ...), condition=%wide.region_14.15_spmd.clone.clone, body=%wide.region_12.14_spmd.clone.clone.sunk | while | flops 101130752 | bytes 1962773 | solution.py:88
  243.8 38.1 %all-gather.11.cloned.1.call-done = f32[256,128,128]{2,1,0:T(8,128)} async-done(((f32[8,128,128]{2,1,0:T(8,128)}), f32[256,128,128]{2,1,0:T(8,128)}) %all-gather.11.cloned.1.call-update) | async-done | bytes 16777232 | tf_op jit(solution)/shard_map/all_gather | solution.py:16
  281.9 74.2 %all-gather.13.cloned.1.call-done = f32[256,128,128]{2,1,0:T(8,128)} async-done(((f32[8,128,128]{2,1,0:T(8,128)}), f32[256,128,128]{2,1,0:T(8,128)}) %all-gather.13.cloned.1.call-update) | async-done | bytes 16777232 | tf_op jit(solution)/shard_map/all_gather | solution.py:16
  356.1 61.2 %while.147 = (s32[]{:T(128)}, f32[8,128,128]{2,1,0:T(8,128)S(1)}, s32[]{:T(128)}, f32[32,8,128,128]{3,2,1,0:T(8,128)}, f32[32,8,128,128]{3,2,1,0:T(8,128)}, /*index=5*/s32[]{:T(128)}, s32[]{:T(128)}) while((s32[]{:T(128)}, f32[8,128,128]{2,1,0:T(8,128)S(1)}, s32[]{:T(128)}, f32[32,8,128,128]{3,2,1,0:T(8,128)}, ...), condition=%wide.region_5.6_spmd.clone, body=%wide.region_4.5_spmd.clone.sunk | while | flops 201850880 | bytes 3672671 | solution.py:28
  426.2 213.1 %while.146 = (s32[]{:T(128)}, f32[8,128,128]{2,1,0:T(8,128)S(1)}, f32[4,8,64,128]{3,2,0,1:T(8,128)}, f32[4,8,64,64]{3,2,1,0:T(8,128)}, f32[4,8,1,64]{3,1,2,0:T(8...) while((s32[]{:T(128)}, f32[8,128,128]{2,1,0:T(8,128)S(1)}, ...), condition=%wide.region_9.10_spmd.clone.clone, body=%wide.region_7.9_spmd.clone.clone.sunk | while | flops 504682560 | bytes 10607041 | solution.py:88
  430.0 40.0 %custom-call.42 = f32[8,1,64,64]{2,3,1,0:T(8,128)} custom-call(f32[8,1,64,64]{3,2,1,0:T(8,128)S(1)} %add_bitcast_fusion.5), custom_call_target="InvertDiagBlocksLowerTriangular" | custom-call | tf_op jit(solution)/shard_map/jvp()/while/body/eval_jaxpr/triangular_solve | solution.py:53
  483.3 40.0 %custom-call.42 = f32[8,1,64,64]{2,3,1,0:T(8,128)} custom-call(f32[8,1,64,64]{3,2,1,0:T(8,128)S(1)} %add_bitcast_fusion.5), custom_call_target="InvertDiagBlocksLowerTriangular" | custom-call | tf_op jit(solution)/shard_map/jvp()/while/body/eval_jaxpr/triangular_solve | solution.py:53
  536.5 40.0 %custom-call.42 = f32[8,1,64,64]{2,3,1,0:T(8,128)} custom-call(f32[8,1,64,64]{3,2,1,0:T(8,128)S(1)} %add_bitcast_fusion.5), custom_call_target="InvertDiagBlocksLowerTriangular" | custom-call | tf_op jit(solution)/shard_map/jvp()/while/body/eval_jaxpr/triangular_solve | solution.py:53
  589.8 40.0 %custom-call.42 = f32[8,1,64,64]{2,3,1,0:T(8,128)} custom-call(f32[8,1,64,64]{3,2,1,0:T(8,128)S(1)} %add_bitcast_fusion.5), custom_call_target="InvertDiagBlocksLowerTriangular" | custom-call | tf_op jit(solution)/shard_map/jvp()/while/body/eval_jaxpr/triangular_solve | solution.py:53
  645.8 212.8 %while.148 = (s32[]{:T(128)}, f32[8,128,128]{2,1,0:T(8,128)}, f32[4,8,64,128]{3,2,1,0:T(8,128)}, f32[4,8,64,1]{2,1,3,0:T(8,128)}, f32[4,8,64,128]{3,2,1,0:T(8,12...) while((s32[]{:T(128)}, f32[8,128,128]{2,1,0:T(8,128)}, ...), condition=%wide.region_16.18_spmd.clone, body=%wide.region_15.17_spmd.clone.sunk | while | flops 403648576 | bytes 6215399 | solution.py:88
  651.7 40.7 %custom-call.43 = f32[8,1,64,64]{2,3,1,0:T(8,128)} custom-call(f32[8,1,64,64]{3,2,1,0:T(8,128)} %fusion.400), custom_call_target="InvertDiagBlocksLowerTriangular" | custom-call | tf_op jit(solution)/shard_map/transpose(jvp())/while/body/eval_jaxpr/triangular_solve/custom-call.2 | solution.py:53
  704.8 40.7 %custom-call.43 = f32[8,1,64,64]{2,3,1,0:T(8,128)} custom-call(f32[8,1,64,64]{3,2,1,0:T(8,128)} %fusion.400), custom_call_target="InvertDiagBlocksLowerTriangular" | custom-call | tf_op jit(solution)/shard_map/transpose(jvp())/while/body/eval_jaxpr/triangular_solve/custom-call.2 | solution.py:53
  757.9 40.7 %custom-call.43 = f32[8,1,64,64]{2,3,1,0:T(8,128)} custom-call(f32[8,1,64,64]{3,2,1,0:T(8,128)} %fusion.400), custom_call_target="InvertDiagBlocksLowerTriangular" | custom-call | tf_op jit(solution)/shard_map/transpose(jvp())/while/body/eval_jaxpr/triangular_solve/custom-call.2 | solution.py:53
  811.1 40.7 %custom-call.43 = f32[8,1,64,64]{2,3,1,0:T(8,128)} custom-call(f32[8,1,64,64]{3,2,1,0:T(8,128)} %fusion.400), custom_call_target="InvertDiagBlocksLowerTriangular" | custom-call | tf_op jit(solution)/shard_map/transpose(jvp())/while/body/eval_jaxpr/triangular_solve/custom-call.2 | solution.py:53
  862.2 11.8 rev.6
  875.9 13.3 psum.22
  893.2 37.8 %all-gather.15.cloned.1.call-done = f32[256,128,128]{2,1,0:T(8,128)} async-done(((f32[8,128,128]{2,1,0:T(8,128)}), f32[256,128,128]{2,1,0:T(8,128)}) %all-gather.15.cloned.1.call-update) | async-done | bytes 16777232 | tf_op jit(solution)/shard_map/all_gather | solution.py:16
  942.7 60.5 %while.149 = (s32[]{:T(128)}, f32[8,128,128]{2,1,0:T(8,128)S(1)}, s32[]{:T(128)}, f32[32,8,128,128]{3,2,1,0:T(8,128)}, f32[32,8,128,128]{3,2,1,0:T(8,128)}, /*index=5*/s32[]{:T(128)}, s32[]{:T(128)}) while((s32[]{:T(128)}, f32[8,128,128]{2,1,0:T(8,128)S(1)}, s32[]{:T(128)}, f32[32,8,128,128]{3,2,1,0:T(8,128)}, ...), condition=%wide.region_18.20_spmd.clone, body=%wide.region_17.19_spmd.clone.sunk | while | flops 201850880 | bytes 3672671 | solution.py:28
  1006.5 453.7 %while.144 = (s32[]{:T(128)}, f32[8,128,128]{2,1,0:T(8,128)S(1)}, f32[4,8,64,128]{3,2,0,1:T(8,128)}, f32[4,8,64,128]{3,2,0,1:T(8,128)}, f32[4,8,64,128]{3,2,0,1:...) while((s32[]{:T(128)}, f32[8,128,128]{2,1,0:T(8,128)S(1)}, ...), condition=%wide.region_23.25_spmd.clone, body=%wide.region_19.24_spmd.clone.sunk | while | flops 1033842752 | bytes 17843592 | solution.py:88
  1011.0 40.0 %custom-call.40 = f32[8,1,64,64]{2,3,1,0:T(8,128)} custom-call(f32[8,1,64,64]{3,2,1,0:T(8,128)S(1)} %fusion.361), custom_call_target="InvertDiagBlocksLowerTriangular" | custom-call | tf_op jit(solution)/shard_map/transpose(jvp())/while/body/eval_jaxpr/triangular_solve/custom-call.2 | solution.py:53
  1065.9 40.0 %custom-call.41 = f32[8,1,64,64]{2,3,1,0:T(8,128)} custom-call(f32[8,1,64,64]{3,2,1,0:T(8,128)S(1)} %add_bitcast_fusion.4), custom_call_target="InvertDiagBlocksLowerTriangular" | custom-call | tf_op jit(solution)/shard_map/transpose(jvp())/while/body/eval_jaxpr/triangular_solve | solution.py:53
  1124.2 40.0 %custom-call.40 = f32[8,1,64,64]{2,3,1,0:T(8,128)} custom-call(f32[8,1,64,64]{3,2,1,0:T(8,128)S(1)} %fusion.361), custom_call_target="InvertDiagBlocksLowerTriangular" | custom-call | tf_op jit(solution)/shard_map/transpose(jvp())/while/body/eval_jaxpr/triangular_solve/custom-call.2 | solution.py:53
  1179.1 40.0 %custom-call.41 = f32[8,1,64,64]{2,3,1,0:T(8,128)} custom-call(f32[8,1,64,64]{3,2,1,0:T(8,128)S(1)} %add_bitcast_fusion.4), custom_call_target="InvertDiagBlocksLowerTriangular" | custom-call | tf_op jit(solution)/shard_map/transpose(jvp())/while/body/eval_jaxpr/triangular_solve | solution.py:53
  1237.5 40.0 %custom-call.40 = f32[8,1,64,64]{2,3,1,0:T(8,128)} custom-call(f32[8,1,64,64]{3,2,1,0:T(8,128)S(1)} %fusion.361), custom_call_target="InvertDiagBlocksLowerTriangular" | custom-call | tf_op jit(solution)/shard_map/transpose(jvp())/while/body/eval_jaxpr/triangular_solve/custom-call.2 | solution.py:53
  1292.5 40.0 %custom-call.41 = f32[8,1,64,64]{2,3,1,0:T(8,128)} custom-call(f32[8,1,64,64]{3,2,1,0:T(8,128)S(1)} %add_bitcast_fusion.4), custom_call_target="InvertDiagBlocksLowerTriangular" | custom-call | tf_op jit(solution)/shard_map/transpose(jvp())/while/body/eval_jaxpr/triangular_solve | solution.py:53
  1350.9 40.0 %custom-call.40 = f32[8,1,64,64]{2,3,1,0:T(8,128)} custom-call(f32[8,1,64,64]{3,2,1,0:T(8,128)S(1)} %fusion.361), custom_call_target="InvertDiagBlocksLowerTriangular" | custom-call | tf_op jit(solution)/shard_map/transpose(jvp())/while/body/eval_jaxpr/triangular_solve/custom-call.2 | solution.py:53
  1405.8 40.0 %custom-call.41 = f32[8,1,64,64]{2,3,1,0:T(8,128)} custom-call(f32[8,1,64,64]{3,2,1,0:T(8,128)S(1)} %add_bitcast_fusion.4), custom_call_target="InvertDiagBlocksLowerTriangular" | custom-call | tf_op jit(solution)/shard_map/transpose(jvp())/while/body/eval_jaxpr/triangular_solve | solution.py:53
  (609 shorter events, 493.6 us)
Async XLA Ops:
  7.2 203.3 %copy-start = (bf16[256,2048]{1,0:T(8,128)(2,1)S(1)}, bf16[256,2048]{1,0:T(8,128)(2,1)}, u32[]{:S(2)}) copy-start(bf16[256,2048]{1,0:T(8,128)(2,1)} %param.37) | copy-start | bytes 3145732
  7.2 4.4 copy-start.26
  7.2 4.5 copy-start.25
  7.2 4.6 copy-start.12
  7.2 274.7 %all-gather.11.cloned.1.call-start = ((), (), s32[]{:S(2)}) async-start(), calls=%async_computation.1 | async-start | bytes 17301504 | tf_op jit(solution)/shard_map/all_gather | solution.py:16
  10.7 197.6 %copy-start.28 = (s32[8]{0:T(128)}, s32[8]{0:T(128)S(1)}, u32[]{:S(2)}) copy-start(s32[8]{0:T(128)S(1)} %and_select_fusion) | copy-start | bytes 100
  200.2 7.3 copy-start.13
  205.7 150.3 %all-gather.13.cloned.1.call-start = ((), (), s32[]{:S(2)}) async-start(), calls=%async_computation.2 | async-start | bytes 17301504 | tf_op jit(solution)/shard_map/all_gather | solution.py:16
  206.6 655.6 %all-gather.9.cloned.1.call-start = ((), (), s32[]{:S(2)}) async-start(), calls=%async_computation | async-start | bytes 17301504 | tf_op jit(solution)/shard_map/all_gather | solution.py:16
  207.4 723.6 %all-gather.15.cloned.1.call-start = ((), (), s32[]{:S(2)}) async-start(), calls=%async_computation.3 | async-start | bytes 17301504 | tf_op jit(solution)/shard_map/all_gather | solution.py:16
  207.7 6.9 copy-start.5
  208.1 6.5 copy-start.22
  208.3 6.3 copy-start.10
  212.3 28.2 %copy-start.15 = (f32[256,16]{0,1:T(8,128)}, f32[256,16]{0,1:T(8,128)S(1)}, u32[]{:S(2)}) copy-start(f32[256,16]{0,1:T(8,128)S(1)} %fusion.227) | copy-start | bytes 49156
  218.5 22.0 %copy-start.14 = (f32[16,1024]{1,0:T(8,128)S(1)}, f32[16,1024]{1,0:T(8,128)}, u32[]{:S(2)}) copy-start(f32[16,1024]{1,0:T(8,128)} %param.35) | copy-start | bytes 196612
  240.5 115.6 %copy-start.31 = (f32[4,8,1,1]{1,3,2,0:T(1,128)}, f32[4,8,1,1]{1,3,2,0:T(1,128)S(1)}, u32[]{:S(2)}) copy-start(f32[4,8,1,1]{1,3,2,0:T(1,128)S(1)} %get-tuple-element.3272) | copy-start | bytes 388
  417.3 8.9 copy-start.23
  426.2 214.8 %copy-start.27 = (f32[128]{0:T(128)S(1)}, f32[128]{0:T(128)}, u32[]{:S(2)}) copy-start(f32[128]{0:T(128)} %param.33) | copy-start | bytes 1540
  639.3 6.5 copy-start.17
  639.3 6.5 copy-start.18
  639.3 6.5 copy-start.19
  639.3 6.5 copy-start.24
  639.3 6.5 copy-start.30
  858.6 621.9 %all-reduce.5.cloned.1.call-start = ((), (), s32[]{:S(2)}) async-start(), calls=%async_computation.4 | async-start | bytes 393216 | tf_op jit(solution)/shard_map/psum | solution.py:197
  862.2 26.9 %copy-start.16 = (f32[256,16]{0,1:T(8,128)S(1)}, f32[256,16]{0,1:T(8,128)}, u32[]{:S(2)}) copy-start(f32[256,16]{0,1:T(8,128)} %copy-done.15) | copy-start | bytes 49156
  1006.5 453.7 %copy-start.29 = (s32[8]{0:T(128)S(1)}, s32[8]{0:T(128)}, u32[]{:S(2)}) copy-start(s32[8]{0:T(128)} %copy-done.28) | copy-start | bytes 100
  1006.5 457.3 %copy-start.21 = (f32[256,4]{0,1:T(4,128)S(1)}, f32[256,4]{0,1:T(4,128)}, u32[]{:S(2)}) copy-start(f32[256,4]{0,1:T(4,128)} %copy-done.20) | copy-start | bytes 12292
  1460.2 5.1 copy-start.6
  1460.2 13.0 copy-start.3
  1460.2 13.0 copy-start.9
  1460.2 14.6 copy-start.11
  1465.2 12.9 copy-start.7
  (6 other events, 11.6 us)
Sparse Core Ops, SparseCore 0:
  205.8 75.9 all-gather.10
  284.1 71.8 all-gather.12
  358.9 72.3 all-gather.8
  858.7 72.2 all-gather.14
  934.8 99.1 all-reduce.4
where the time goes:
time: 1510 us; the launch traced here: 1490 us
  other arithmetic  847 us (56%)
  matrix products  368 us (24%)
  waiting for transfers between devices  151 us (10%)
  local copies, waits for them, and re-layouts  91.2 us (6%)
    another operation x72, other arithmetic, block_step(): lax.linalg.triangular_solve(identity + strict_part, targets, left_side=Tr...  819 us
    all_gather x4, waiting for transfers between devices, prefix(): pieces = jax.tree.map(lambda part: lax.all_gather(part, axis), value)  150 us
    dot_general x62, matrix products, compose(): jnp.einsum('hij,hjk->hik', second_part[0], first_part[1], precision=fines...  117 us
    dot_general x20, matrix products, block_step(): jnp.einsum('hcd,hdw->hcw', key_block, state, precision=finest_precision)  36.4 us
    dot_general x16, matrix products, block_step(): jnp.einsum('hcd,hed->hce', query_block, key_block, precision=finest_preci...  33.7 us
    dot_general x20, matrix products, block_step(): jnp.einsum('hcd,hcw->hdw', key_block * weight, deltas, precision=finest_p...  32.6 us
    dot_general x16, matrix products, block_step(): jnp.einsum('hcd,hdw->hcw', query_block, state, precision=finest_precision)  32.4 us
    another operation x20, matrix products, block_step(): lax.linalg.triangular_solve(identity + strict_part, targets, left_side=Tr...  31.3 us
  transfers between devices with their start and end apart: 5, of which 3 were waited for; matrix products, arithmetic and copies ran while one was open for 74% of the time, Pallas kernels for 0%

commit v1 on v0

v1 whole, which is shorter than its diff:
```python
import functools

import jax
import jax.numpy as jnp
from jax import lax
from jax.experimental import pallas as pl
from jax.experimental.pallas import tpu as pltpu
from jax.sharding import PartitionSpec as P

DK = 128
DV = 128
TOK = 256
HALF = 128
HEADS = 8
KEYS = 4
RANK = 16
EPS = 1e-06
F32 = jnp.float32
BF16 = jnp.bfloat16
MESH = pl.DeviceIdType.MESH

NN = (((1,), (0,)), ((), ()))
NT = (((1,), (1,)), ((), ()))
TN = (((0,), (0,)), ((), ()))


def dot(x, y, form=NN):
    return lax.dot_general(x, y, form, preferred_element_type=F32)


def split(x):
    high = x.astype(BF16)
    return high, (x - high.astype(F32)).astype(BF16)


def cat(parts, axis):
    return jnp.concatenate(parts, axis=axis)


def dot3(x, y, form=NN):
    cx, cy = form[0][0][0], form[0][1][0]
    return dot(cat([x[0], x[1], x[0]], cx), cat([y[0], y[0], y[1]], cy), form)


def dot2(x, exact, form=NN):
    cx, cy = form[0][0][0], form[0][1][0]
    return dot(cat(list(x), cx), cat([exact, exact], cy), form)


def dot2r(exact, y, form=NN):
    cx, cy = form[0][0][0], form[0][1][0]
    return dot(cat([exact, exact], cx), cat(list(y), cy), form)


def square(x, y):
    right = cat([cat([y[0], y[1]], 1), cat([y[0], jnp.zeros_like(y[1])], 1)], 0)
    both = dot(cat([x[0], x[1]], 1), right)
    return both[:, :HALF] + both[:, HALF:]


def grid_of(rows, columns):
    return (
        lax.broadcasted_iota(jnp.int32, (rows, columns), 0),
        lax.broadcasted_iota(jnp.int32, (rows, columns), 1),
    )


def inverses(blocks):
    row, col = grid_of(HALF, HALF)
    eye = jnp.where(row == col, 1.0, 0.0).astype(F32)
    pairs = ((row >> 1) == (col >> 1)) & (row > col)
    found = [eye - jnp.where(pairs, block, 0.0) for block in blocks]
    for level in range(1, 7):
        here = ((row >> (level + 1)) == (col >> (level + 1))) & ((row >> level) > (col >> level))
        halves = [split(x) for x in found]
        inner = [
            split(square(split(jnp.where(here, block, 0.0)), x))
            for block, x in zip(blocks, halves)
        ]
        found = [x - square(h, y) for x, h, y in zip(found, halves, inner)]
    return found


ROW_R, ROW_C, ROW_P, ROW_G, ROW_BG, ROW_AG, ROW_KEY = 0, 8, 16, 24, 32, 40, 48


def local_kernel(
    which,
    q_ref,
    k_ref,
    v_ref,
    rate_ref,
    code_ref,
    og_ref,
    weight_ref,
    lower_ref,
    raise_ref,
    a_ref,
    bt_ref,
    w_ref,
    u_ref,
    e_ref,
    o_ref,
    zt_ref,
    yh_ref,
    yl_ref,
    gn_ref,
    gr_ref,
    rows_ref,
    cols_ref,
    k4,
    kt4,
    q4,
    kk4,
    qk4,
):
    lane = lax.broadcasted_iota(jnp.int32, (HEADS, TOK), 1)
    gamma = 1.0 - code_ref[...].astype(F32) * 2.0 ** (-20)
    step = 1
    while step < TOK:
        gamma = gamma * jnp.where(lane >= step, pltpu.roll(gamma, step, 1), 1.0)
        step *= 2
    back = 1.0 / gamma
    ones = jnp.ones((8, DK), BF16)
    rows_ref[...] = jnp.zeros_like(rows_ref)
    for m in range(KEYS):
        at = slice(m * DK, (m + 1) * DK)
        k = k_ref[:, at]
        q = q_ref[:, at]
        k4[m] = k
        q4[m] = q
        kt4[m] = k.T
        kk4[m] = dot(k, k, NT)
        qk4[m] = dot(q, k, NT)
        kf, qf = k.astype(F32), q.astype(F32)
        ksum = dot2r(ones, split(kf * kf), NT)[0:1]
        qsum = dot2r(ones, split(qf * qf), NT)[0:1]
        rows_ref[ROW_KEY + m : ROW_KEY + m + 1, :] = lax.rsqrt(ksum + EPS)
        rows_ref[ROW_KEY + KEYS + m : ROW_KEY + KEYS + m + 1, :] = lax.rsqrt(qsum + EPS)
    rate = rate_ref[...]
    for h in range(HEADS):
        m = which[h] % KEYS
        a = rows_ref[pl.ds(ROW_KEY + m, 1), :]
        b = rows_ref[pl.ds(ROW_KEY + KEYS + m, 1), :] * DK ** (-0.5)
        g, i, r = gamma[h : h + 1], back[h : h + 1], rate[h : h + 1]
        for at, value in (
            (ROW_R, g * a),
            (ROW_C, a * r * i),
            (ROW_P, g * b),
            (ROW_G, g),
            (ROW_BG, r * i),
            (ROW_AG, a * i),
        ):
            rows_ref[at + h : at + h + 1, :] = value
    cols_ref[...] = rows_ref[...].T
    row, col = grid_of(TOK, TOK)
    srow, scol = grid_of(HALF, HALF)
    eye = jnp.where(srow == scol, 1.0, 0.0).astype(F32)

    def column(at):
        return cols_ref[:, at : at + 1]

    def line(at):
        return rows_ref[at : at + 1, :]

    group = 4
    for start in range(0, HEADS, group):
        heads = range(start, start + group)
        keys = [which[h] % KEYS for h in heads]
        blocks, corners = [], []
        for h, m in zip(heads, keys):
            strict = jnp.where(row > col, kk4[m] * column(ROW_R + h) * line(ROW_C + h), 0.0)
            blocks += [strict[:HALF, :HALF], strict[HALF:, HALF:]]
            corners.append(split(strict[HALF:, :HALF]))
        found = inverses(blocks)
        for n, (h, m) in enumerate(zip(heads, keys)):
            first, second = split(found[2 * n]), split(found[2 * n + 1])
            corner = split(-square(second, split(square(corners[n], first))))
            blank = jnp.zeros((HALF, HALF), BF16)
            t = tuple(
                cat([cat([first[i], blank], 1), cat([corner[i], second[i]], 1)], 0)
                for i in range(2)
            )
            k, q = k4[m].astype(F32), q4[m].astype(F32)
            v = v_ref[:, h * DV : (h + 1) * DV]
            last = rows_ref[ROW_G + h : ROW_G + h + 1, TOK - 1 : TOK]
            ended = split(kt4[m].astype(F32) * (line(ROW_C + h) * last))
            zt = dot3(ended, t)
            zs = split(zt)
            scaled = k * column(ROW_R + h)
            g = split(scaled)
            zt_ref[h] = zt
            a_ref[h] = last * eye - dot3(zs, g)
            bt_ref[h] = dot2r(v.T, zs, NT)
            pair = cat([g[0], v], 1)
            wu = dot2(t, pair)
            w_ref[h] = wu[:, :DK] + dot(t[0], g[1])
            u_ref[h] = wu[:, DK:]
            mixing = jnp.where(row >= col, qk4[m] * column(ROW_P + h) * line(ROW_C + h), 0.0)
            y = split(dot3(split(mixing), t))
            yh_ref[h] = y[0]
            yl_ref[h] = y[1]
            eo = dot2(y, pair)
            e_ref[h] = q * column(ROW_P + h) - (eo[:, :DK] + dot(y[0], g[1]))
            o_ref[h] = eo[:, DK:]
    rs = split(raise_ref[...])
    both = dot(cat(list(rs), 0), og_ref[...], NT)
    grt = both[:RANK] + both[RANK:]
    gr_ref[...] = grt
    gs = split(2.0 * grt)
    for h in range(HEADS):
        at = slice(h * DV, (h + 1) * DV)
        low = dot3(gs, split(lower_ref[:, at]), TN)
        gn_ref[:, at] = dot(og_ref[...], weight_ref[at, :], NT) + low


def middle_kernel(
    which,
    s0_ref,
    q_ref,
    k_ref,
    w_ref,
    u_ref,
    e_ref,
    o_ref,
    yh_ref,
    yl_ref,
    gn_ref,
    gr_ref,
    rows_ref,
    cols_ref,
    gain_ref,
    og_ref,
    lower_ref,
    ct_ref,
    xt_ref,
    uf_ref,
    ft_ref,
    dq_ref,
    down_ref,
    raise_ref,
    k4,
    q4,
    qt4,
    acc4,
):
    for m in range(KEYS):
        at = slice(m * DK, (m + 1) * DK)
        k4[m] = k_ref[:, at]
        q4[m] = q_ref[:, at]
        qt4[m] = q_ref[:, at].T
    acc4[...] = jnp.zeros_like(acc4)
    row, col = grid_of(TOK, TOK)
    gain = gain_ref[...]
    gs = split(2.0 * gr_ref[...])
    rank = jnp.zeros((RANK, TOK), F32)
    for h in range(HEADS):
        m = which[h] % KEYS
        at = slice(h * DV, (h + 1) * DV)
        ss = split(s0_ref[h])
        es = split(e_ref[h])
        ws = split(w_ref[h])
        o = o_ref[h] + dot3(es, ss, NT)
        u = u_ref[h] - dot3(ws, ss, NT)
        uf_ref[h] = u
        r = lax.rsqrt(jnp.mean(o * o, axis=-1, keepdims=True) + EPS)
        gn = gn_ref[:, at] * gain
        tail = jnp.mean(gn * o, axis=-1, keepdims=True)
        do = r * gn - o * (r * r * r * tail)
        normed = split(o * r * gain)
        dts = split(do.T)
        ct_ref[h] = dot3(dts, es)
        xt_ref[h] = dot3(dts, (yh_ref[h], yl_ref[h]))
        rank = rank + dot3(split(lower_ref[:, at]), normed, NT)
        down_ref[:, at] = dot3(gs, normed)
        ds, us = split(do), split(u)
        dp = split(jnp.where(row >= col, dot3(ds, us, NT), 0.0))
        ck = split(k4[m].astype(F32) * cols_ref[:, ROW_C + h : ROW_C + h + 1])
        dqh = (dot3(ds, ss) + dot3(dp, ck)) * cols_ref[:, ROW_G + h : ROW_G + h + 1]
        pq = split(qt4[m].astype(F32) * rows_ref[ROW_P + h : ROW_P + h + 1, :])
        ft_ref[h] = dot3(pq, dp)
        acc4[m] = acc4[m] + dqh
    raise_ref[...] = 2.0 * dot2(split(rank), og_ref[...])
    for m in range(KEYS):
        total = acc4[m]
        q = q4[m].astype(F32)
        inv = cols_ref[:, ROW_KEY + KEYS + m : ROW_KEY + KEYS + m + 1]
        along = jnp.sum(total * q, axis=-1, keepdims=True)
        dq_ref[:, m * DK : (m + 1) * DK] = (DK ** (-0.5) * inv) * (total - q * (inv * inv * along))


def last_kernel(
    which,
    ds_ref,
    s0_ref,
    k_ref,
    xt_ref,
    zt_ref,
    u_ref,
    ft_ref,
    rows_ref,
    cols_ref,
    dk_ref,
    dv_ref,
    db_ref,
    k4,
    kt4,
    acc4,
    acct4,
):
    for m in range(KEYS):
        at = slice(m * DK, (m + 1) * DK)
        k4[m] = k_ref[:, at]
        kt4[m] = k_ref[:, at].T
    acc4[...] = jnp.zeros_like(acc4)
    acct4[...] = jnp.zeros_like(acct4)
    row, col = grid_of(TOK, TOK)
    for h in range(HEADS):
        m = which[h] % KEYS
        dst = ds_ref[h]
        drt = xt_ref[h] + dot3(split(dst), split(zt_ref[h]))
        dr = drt.T
        dv_ref[:, h * DV : (h + 1) * DV] = dr
        drs, us = split(dr), split(u_ref[h])
        dl = split(jnp.where(row > col, -dot3(drs, us, NT), 0.0))
        kt = kt4[m].astype(F32)
        rk = split(kt * rows_ref[ROW_R + h : ROW_R + h + 1, :])
        ck = split(k4[m].astype(F32) * cols_ref[:, ROW_C + h : ROW_C + h + 1])
        last = rows_ref[ROW_G + h : ROW_G + h + 1, TOK - 1 : TOK]
        f = ft_ref[h] + dot3(rk, dl) + last * dot3(split(dst.T), us, NT)
        db_ref[h : h + 1, :] = (
            jnp.sum(kt * f, axis=0, keepdims=True) * rows_ref[ROW_AG + h : ROW_AG + h + 1, :]
        )
        own = dot3(dl, ck) - dot3(drs, split(s0_ref[h]))
        acc4[m] = acc4[m] + own * cols_ref[:, ROW_G + h : ROW_G + h + 1]
        acct4[m] = acct4[m] + f * rows_ref[ROW_BG + h : ROW_BG + h + 1, :]
    for m in range(KEYS):
        total = acc4[m] + acct4[m].T
        k = k4[m].astype(F32)
        inv = cols_ref[:, ROW_KEY + m : ROW_KEY + m + 1]
        along = jnp.sum(total * k, axis=-1, keepdims=True)
        dk_ref[:, m * DK : (m + 1) * DK] = inv * (total - k * (inv * inv * along))


def greet(count, me):
    barrier = pltpu.get_barrier_semaphore()

    def one(s, carry):
        other = lax.rem(me + s, count)
        pl.semaphore_signal(barrier, inc=1, device_id={"seq": other}, device_id_type=MESH)
        return carry

    lax.fori_loop(1, count, one, 0)
    pl.semaphore_wait(barrier, count - 1)


def scan_kernel(count, backward, *refs):
    if backward:
        b_ref, all_ref, s_ref, bbuf, sbuf, send_sem, b_sem, s_sem = refs
    else:
        a_ref, b_ref, s_ref, all_ref, bbuf, sbuf, send_sem, b_sem, s_sem, a_sem, asend_sem = refs
    me = lax.axis_index("seq")
    rows = HEADS * DV // count
    per = DV // rows

    def piece(ref, owner):
        head = owner // per
        return ref.at[head, pl.ds(pl.multiple_of(lax.rem(owner, per) * rows, rows), rows)]

    def remote(src, dst, ssem, rsem, other):
        return pltpu.make_async_remote_copy(
            src_ref=src,
            dst_ref=dst,
            send_sem=ssem,
            recv_sem=rsem,
            device_id={"seq": other},
            device_id_type=MESH,
        )

    def arrived(ref, sem):
        pltpu.make_async_copy(ref, ref, sem).wait()

    own_b = pltpu.make_async_copy(piece(b_ref, me), bbuf.at[me], b_sem.at[me])
    own_b.start()
    if not backward:
        own_a = pltpu.make_async_copy(a_ref.at[me // per], all_ref.at[me], a_sem.at[me])
        own_a.start()
    greet(count, me)

    def deal(s, carry):
        other = lax.rem(me + s, count)
        if not backward:
            remote(
                a_ref.at[other // per], all_ref.at[me], asend_sem.at[other], a_sem.at[me], other
            ).start()
        remote(
            piece(b_ref, other), bbuf.at[me], send_sem.at[other], b_sem.at[me], other
        ).start()
        return carry

    lax.fori_loop(1, count, deal, 0)

    sbuf[0] = jnp.zeros((rows, DK), F32)

    def turn(t, carry):
        j = count - 1 - t if backward else t

        @pl.when(j == me)
        def _():
            pltpu.make_async_copy(sbuf.at[t], piece(s_ref, me), s_sem.at[me]).start()

        @pl.when(j != me)
        def _():
            remote(
                sbuf.at[t], piece(s_ref, me), send_sem.at[count + j], s_sem.at[me], j
            ).start()

        arrived(bbuf.at[j], b_sem.at[j])
        if not backward:
            arrived(all_ref.at[j], a_sem.at[j])
        form = NN if backward else NT
        sbuf[t + 1] = dot3(split(sbuf[t]), split(all_ref[j]), form) + bbuf[j]
        return carry

    lax.fori_loop(0, count, turn, 0)

    def settle(s, carry):
        other = lax.rem(me + s, count)
        arrived(piece(b_ref, other), send_sem.at[other])
        arrived(sbuf.at[other], send_sem.at[count + other])
        if not backward:
            arrived(a_ref.at[other // per], asend_sem.at[other])
        arrived(piece(s_ref, other), s_sem.at[other])
        return carry

    lax.fori_loop(1, count, settle, 0)
    arrived(piece(s_ref, me), s_sem.at[me])


VM = pl.BlockSpec(memory_space=pltpu.VMEM)
SM = pl.BlockSpec(memory_space=pltpu.SMEM)
LIMIT = 56 * 1024 * 1024


def struct(*shape, dtype=F32):
    return jax.ShapeDtypeStruct(shape, dtype)


def forward_scan(a, bt, count):
    rows = HEADS * DV // count
    return pl.pallas_call(
        functools.partial(scan_kernel, count, False),
        out_shape=(struct(HEADS, DV, DK), struct(count, DK, DK)),
        in_specs=[VM] * 2,
        out_specs=(VM, VM),
        scratch_shapes=[
            pltpu.VMEM((count, rows, DK), F32),
            pltpu.VMEM((count + 1, rows, DK), F32),
            pltpu.SemaphoreType.DMA((2 * count,)),
            pltpu.SemaphoreType.DMA((count,)),
            pltpu.SemaphoreType.DMA((count,)),
            pltpu.SemaphoreType.DMA((count,)),
            pltpu.SemaphoreType.DMA((count,)),
        ],
        compiler_params=pltpu.CompilerParams(
            collective_id=0, has_side_effects=True, vmem_limit_bytes=LIMIT
        ),
        name="forward_states",
    )(a, bt)


def backward_scan(ct, everyone, count):
    rows = HEADS * DV // count
    return pl.pallas_call(
        functools.partial(scan_kernel, count, True),
        out_shape=struct(HEADS, DV, DK),
        in_specs=[VM] * 2,
        out_specs=VM,
        scratch_shapes=[
            pltpu.VMEM((count, rows, DK), F32),
            pltpu.VMEM((count + 1, rows, DK), F32),
            pltpu.SemaphoreType.DMA((2 * count,)),
            pltpu.SemaphoreType.DMA((count,)),
            pltpu.SemaphoreType.DMA((count,)),
        ],
        compiler_params=pltpu.CompilerParams(
            collective_id=1, has_side_effects=True, vmem_limit_bytes=LIMIT
        ),
        name="state_gradients",
    )(ct, everyone)


def body(
    query_matrix_rows,
    key_matrix_rows,
    value_matrix_rows,
    write_strength,
    forget_gate_code,
    value_to_key_head,
    output_norm_gain,
    output_weight,
    adapter_lowering,
    adapter_raising,
    output_gradient,
):
    count = lax.axis_size("seq")
    params = pltpu.CompilerParams(vmem_limit_bytes=LIMIT)
    per_head = struct(HEADS, TOK, DK)
    a, bt, w, u, e, o, zt, yh, yl, gn, gr, rows, cols = pl.pallas_call(
        local_kernel,
        out_shape=(
            struct(HEADS, DK, DK),
            struct(HEADS, DV, DK),
            per_head,
            per_head,
            per_head,
            per_head,
            struct(HEADS, DK, TOK),
            struct(HEADS, TOK, TOK, dtype=BF16),
            struct(HEADS, TOK, TOK, dtype=BF16),
            struct(TOK, HEADS * DV),
            struct(RANK, TOK),
            struct(128, TOK),
            struct(TOK, 128),
        ),
        in_specs=[SM] + [VM] * 9,
        out_specs=(VM,) * 13,
        scratch_shapes=[
            pltpu.VMEM((KEYS, TOK, DK), BF16),
            pltpu.VMEM((KEYS, DK, TOK), BF16),
            pltpu.VMEM((KEYS, TOK, DK), BF16),
            pltpu.VMEM((KEYS, TOK, TOK), F32),
            pltpu.VMEM((KEYS, TOK, TOK), F32),
        ],
        compiler_params=params,
        name="local_pass",
    )(
        value_to_key_head,
        query_matrix_rows,
        key_matrix_rows,
        value_matrix_rows,
        write_strength,
        forget_gate_code,
        output_gradient,
        output_weight,
        adapter_lowering,
        adapter_raising,
    )
    s0, everyone = forward_scan(a, bt, count)
    ct, xt, uf, ft, dq, down, lift = pl.pallas_call(
        middle_kernel,
        out_shape=(
            struct(HEADS, DV, DK),
            struct(HEADS, DV, TOK),
            per_head,
            struct(HEADS, DK, TOK),
            struct(TOK, KEYS * DK),
            struct(RANK, HEADS * DV),
            struct(RANK, output_gradient.shape[1]),
        ),
        in_specs=[SM] + [VM] * 16,
        out_specs=(VM,) * 7,
        scratch_shapes=[
            pltpu.VMEM((KEYS, TOK, DK), BF16),
            pltpu.VMEM((KEYS, TOK, DK), BF16),
            pltpu.VMEM((KEYS, DK, TOK), BF16),
            pltpu.VMEM((KEYS, TOK, DK), F32),
        ],
        compiler_params=params,
        name="middle_pass",
    )(
        value_to_key_head,
        s0,
        query_matrix_rows,
        key_matrix_rows,
        w,
        u,
        e,
        o,
        yh,
        yl,
        gn,
        gr,
        rows,
        cols,
        output_norm_gain.reshape(1, DV),
        output_gradient,
        adapter_lowering,
    )
    grad_down = lax.psum(down, "seq")
    raising_gradient = lax.psum(lift, ("seq", "head"))
    ds = backward_scan(ct, everyone, count)
    dk, dv, db = pl.pallas_call(
        last_kernel,
        out_shape=(
            struct(TOK, KEYS * DK),
            struct(TOK, HEADS * DV),
            struct(HEADS, TOK),
        ),
        in_specs=[SM] + [VM] * 9,
        out_specs=(VM,) * 3,
        scratch_shapes=[
            pltpu.VMEM((KEYS, TOK, DK), BF16),
            pltpu.VMEM((KEYS, DK, TOK), BF16),
            pltpu.VMEM((KEYS, TOK, DK), F32),
            pltpu.VMEM((KEYS, DK, TOK), F32),
        ],
        compiler_params=params,
        name="last_pass",
    )(value_to_key_head, ds, s0, key_matrix_rows, xt, zt, uf, ft, rows, cols)
    return (dq, dk, dv, db, grad_down, raising_gradient)


def solution(mesh):
    placed = (
        P("seq", "head"),
        P("seq", "head"),
        P("seq", "head"),
        P("head", "seq"),
        P("head", "seq"),
        P("head"),
        P(),
        P("head", None),
        P(None, "head"),
        P(),
        P("seq", None),
    )
    return jax.shard_map(
        body,
        mesh=mesh,
        in_specs=placed,
        out_specs=(
            P("seq", "head"),
            P("seq", "head"),
            P("seq", "head"),
            P("head", "seq"),
            P(None, "head"),
            P(),
        ),
        check_vma=False,
    )
```

time: 1510 us -> 361 us (0.24); the launches traced: 1490 us -> 361 us
  other arithmetic: 847 us -> 0 us
  matrix products: 368 us -> 0 us
  Pallas kernels: 0 us -> 132 us
  local copies, waits for them, and re-layouts: 91.2 us -> 3.04 us
  waiting for transfers between devices: 151 us -> 212 us
    another operation x85 -> x0, other arithmetic: 821 us -> none  [the longest x72 819 us: block_step(): lax.linalg.triangular_solve(identity + strict_part, targets, left_side=Tr...]
    dot_general x184 -> x0, matrix products: 337 us -> none  [the longest x62 117 us: compose(): jnp.einsum('hij,hjk->hik', second_part[0], first_part[1], precision=fines...]
    psum x1 -> x2, waiting for transfers between devices: 0.01 us -> 211 us  [the longest x1 144 us: body(): raising_gradient = lax.psum(lift, ('seq', 'head'))]
    all_gather x4 -> x0, waiting for transfers between devices: 150 us -> none  [prefix(): pieces = jax.tree.map(lambda part: lax.all_gather(part, axis), value)]
    pallas_call x0 -> x5, Pallas kernels: none -> 132 us  [the longest x1 58.7 us: forward_scan(): pl.pallas_call(functools.partial(scan_kernel, count, False), out_shape=(s...]
    another operation x20 -> x0, matrix products: 31.3 us -> none  [block_step(): lax.linalg.triangular_solve(identity + strict_part, targets, left_side=Tr...]
    rev x2 -> x0, local copies, waits for them, and re-layouts: 23.4 us -> none  [prefix(): pieces = jax.tree.map(lambda part: part[::-1], pieces)]
    another operation x21 -> x0, local copies, waits for them, and re-layouts: 16.1 us -> none
  transfers between devices with their start and end apart: 5 -> 2, of which waited for: 3 -> 2; matrix products, arithmetic and copies ran while one was open for 74% -> 0% of each run, Pallas kernels for 0% -> 11%
where the time goes in v1:
time: 361 us
  waiting for transfers between devices  212 us (59%)
  Pallas kernels  132 us (37%)
  between operations  14.1 us (4%)
    psum x1, waiting for transfers between devices, body(): raising_gradient = lax.psum(lift, ('seq', 'head'))  144 us
    psum x1, waiting for transfers between devices, body(): grad_down = lax.psum(down, 'seq')  66.8 us
    pallas_call x1, Pallas kernels, forward_scan(): pl.pallas_call(functools.partial(scan_kernel, count, False), out_shape=(s...  58.7 us
    pallas_call x1, Pallas kernels, backward_scan(): pl.pallas_call(functools.partial(scan_kernel, count, True), out_shape=str...  28.8 us
    pallas_call x1, Pallas kernels, body(): pl.pallas_call(local_kernel, out_shape=(struct(HEADS, DK, DK), struct(HEA...  21.1 us
    pallas_call x1, Pallas kernels, body(): pl.pallas_call(middle_kernel, out_shape=(struct(HEADS, DV, DK), struct(HE...  13.2 us
    pallas_call x1, Pallas kernels, body(): pl.pallas_call(last_kernel, out_shape=(struct(TOK, KEYS * DK), struct(TOK...  9.99 us
  transfers between devices with their start and end apart: 2, of which 2 were waited for; matrix products, arithmetic and copies ran while one was open for 0% of the time, Pallas kernels for 11%

profile of v1, /device:TPU:1, one launch (start us, length us, event | category | flops | bytes accessed | tf_op | source)
XLA Modules:
  0.0 360.7 jit_solution(2259746066805340492)
XLA Ops:
  7.2 0.0 all-reduce.3.cloned.1.call-start
  7.2 21.1 %local_pass.1 = (f32[8,128,128]{2,1,0:T(8,128)}, f32[8,128,128]{2,1,0:T(8,128)}, f32[8,256,128]{2,1,0:T(8,128)}, f32[8,256,128]{2,1,0:T(8,128)}, f32[8,256,128]{...) custom-call(s32[8]{0:T(128)} %which.5, ...), custom_call_target="tpu_custom_call" | custom-call | tf_op jit(solution)/shard_map/local_pass/pallas_call | solution.py:509
  28.3 58.7 %forward_states.1 = (f32[8,128,128]{2,1,0:T(8,128)}, f32[32,128,128]{2,1,0:T(8,128)}) custom-call(f32[8,128,128]{2,1,0:T(8,128)} %get-tuple-element.31.refs_0_, f32[8,128,128]{2,1,0:T(8,128)} %get-tuple-element.32.refs_1_), custom_call_target="tpu_custom_call" | custom-call | tf_op jit(solution)/shard_map/forward_states/pallas_call | solution.py:451
  87.0 13.2 %middle_pass.1 = (f32[8,128,128]{2,1,0:T(8,128)}, f32[8,128,256]{2,1,0:T(8,128)}, f32[8,256,128]{2,1,0:T(8,128)}, f32[8,128,256]{2,1,0:T(8,128)}, f32[256,512]{1...) custom-call(s32[8]{0:T(128)} %which.5, f32[8,128,128]{2,1,0:T(8,128)} %get-tuple-element.33.s0_ref, ...), custom_call_target="tpu_custom_call" | custom-call | tf_op jit(solution)/shard_map/middle_pass/pallas_call | solution.py:550
  100.2 0.0 all-reduce.3.cloned.1.call-update
  100.2 0.3 all-reduce.5.cloned.1.call-start
  100.5 0.5 all-reduce.5.cloned.1.call-update
  101.0 28.8 %state_gradients.1.ds_ref = f32[8,128,128]{2,1,0:T(8,128)} custom-call(f32[8,128,128]{2,1,0:T(8,128)} %get-tuple-element.45.refs_0_, f32[32,128,128]{2,1,0:T(8,128)} %get-tuple-element.46.refs_1_), custom_call_target="tpu_custom_call" | custom-call | tf_op jit(solution)/shard_map/state_gradients/pallas_call | solution.py:474
  129.8 10.0 %last_pass.1 = (f32[256,512]{1,0:T(8,128)}, f32[256,1024]{1,0:T(8,128)}, f32[8,256]{1,0:T(8,128)}) custom-call(s32[8]{0:T(128)} %which.5, f32[8,128,128]{2,1,0:T(8,128)} %state_gradients.1.ds_ref, f32[8,128,128]{2,1,0:T(8,128)} %get-tuple-element.33.s0_ref, bf16[256,512]{1,0:T(8,128)(2,1)} %k_ref.5, f32[8,128,256]{2,1,0:T(8,128)} %get-tuple-element.47.xt_ref, ...), custom_call_target="tpu_custom_call" | custom-call | tf_op jit(solution)/shard_map/last_pass/pallas_call | solution.py:593
  139.7 66.8 %all-reduce.3.cloned.1.call-done = f32[16,1024]{1,0:T(8,128)} async-done(((f32[16,1024]{1,0:T(8,128)}), f32[16,1024]{1,0:T(8,128)}) %all-reduce.3.cloned.1.call-update) | async-done | bytes 65552 | tf_op jit(solution)/shard_map/psum | solution.py:590
  206.5 144.2 %all-reduce.5.cloned.1.call-done = f32[16,2048]{1,0:T(8,128)} async-done(((f32[16,2048]{1,0:T(8,128)}), f32[16,2048]{1,0:T(8,128)}) %all-reduce.5.cloned.1.call-update) | async-done | bytes 131088 | tf_op jit(solution)/shard_map/psum | solution.py:591
  350.8 1.5 copy.19
  352.2 1.6 copy.20
Async XLA Ops:
  7.2 199.4 %all-reduce.3.cloned.1.call-start = ((), (), s32[]{:S(2)}) async-start(), calls=%async_computation | async-start | bytes 131072 | tf_op jit(solution)/shard_map/psum | solution.py:590
  100.2 250.5 %all-reduce.5.cloned.1.call-start = ((), (), s32[]{:S(2)}) async-start(), calls=%async_computation.1 | async-start | bytes 262144 | tf_op jit(solution)/shard_map/psum | solution.py:591
Sparse Core Ops, SparseCore 0:
  100.4 106.1 all-reduce.2
  212.0 138.7 all-reduce.4

commit v2 on v1

--- a/solution.py
+++ b/solution.py
@@ -237,8 +237,7 @@
     uf_ref,
     ft_ref,
     dq_ref,
-    down_ref,
-    raise_ref,
+    red_ref,
     k4,
     q4,
     qt4,
@@ -272,7 +271,7 @@
         ct_ref[h] = dot3(dts, es)
         xt_ref[h] = dot3(dts, (yh_ref[h], yl_ref[h]))
         rank = rank + dot3(split(lower_ref[:, at]), normed, NT)
-        down_ref[:, at] = dot3(gs, normed)
+        red_ref[h] = dot3(gs, normed)
         ds, us = split(do), split(u)
         dp = split(jnp.where(row >= col, dot3(ds, us, NT), 0.0))
         ck = split(k4[m].astype(F32) * cols_ref[:, ROW_C + h : ROW_C + h + 1])
@@ -280,7 +279,9 @@
         pq = split(qt4[m].astype(F32) * rows_ref[ROW_P + h : ROW_P + h + 1, :])
         ft_ref[h] = dot3(pq, dp)
         acc4[m] = acc4[m] + dqh
-    raise_ref[...] = 2.0 * dot2(split(rank), og_ref[...])
+    lift = 2.0 * dot2(split(rank), og_ref[...])
+    for n in range(lift.shape[1] // 128):
+        red_ref[HEADS + n] = lift[:, n * 128 : (n + 1) * 128]
     for m in range(KEYS):
         total = acc4[m]
         q = q4[m].astype(F32)
@@ -300,9 +301,12 @@
     ft_ref,
     rows_ref,
     cols_ref,
+    fin_ref,
     dk_ref,
     dv_ref,
     db_ref,
+    down_ref,
+    raise_ref,
     k4,
     kt4,
     acc4,
@@ -314,6 +318,10 @@
         kt4[m] = k_ref[:, at].T
     acc4[...] = jnp.zeros_like(acc4)
     acct4[...] = jnp.zeros_like(acct4)
+    for n in range(HEADS):
+        down_ref[:, n * 128 : (n + 1) * 128] = fin_ref[n]
+    for n in range(raise_ref.shape[1] // 128):
+        raise_ref[:, n * 128 : (n + 1) * 128] = fin_ref[HEADS + n]
     row, col = grid_of(TOK, TOK)
     for h in range(HEADS):
         m = which[h] % KEYS
@@ -342,99 +350,320 @@
         dk_ref[:, m * DK : (m + 1) * DK] = inv * (total - k * (inv * inv * along))
 
 
-def greet(count, me):
+def remote(src, dst, ssem, rsem, **where):
+    return pltpu.make_async_remote_copy(
+        src_ref=src,
+        dst_ref=dst,
+        send_sem=ssem,
+        recv_sem=rsem,
+        device_id=where,
+        device_id_type=MESH,
+    )
+
+
+def arrived(ref, sem):
+    pltpu.make_async_copy(ref, ref, sem).wait()
+
+
+def greet(count, me, step, extra=()):
     barrier = pltpu.get_barrier_semaphore()
 
     def one(s, carry):
-        other = lax.rem(me + s, count)
+        other = lax.rem(me + s * step, count)
         pl.semaphore_signal(barrier, inc=1, device_id={"seq": other}, device_id_type=MESH)
         return carry
 
-    lax.fori_loop(1, count, one, 0)
-    pl.semaphore_wait(barrier, count - 1)
-
-
-def scan_kernel(count, backward, *refs):
-    if backward:
-        b_ref, all_ref, s_ref, bbuf, sbuf, send_sem, b_sem, s_sem = refs
-    else:
-        a_ref, b_ref, s_ref, all_ref, bbuf, sbuf, send_sem, b_sem, s_sem, a_sem, asend_sem = refs
+    lax.fori_loop(1, count // step, one, 0)
+    for where in extra:
+        pl.semaphore_signal(barrier, inc=1, device_id=where, device_id_type=MESH)
+    pl.semaphore_wait(barrier, count // step - 1 + len(extra))
+
+
+OWN = HEADS // 2
+
+
+def place(count):
     me = lax.axis_index("seq")
-    rows = HEADS * DV // count
+    core = lax.rem(me, 2)
+    return me, me // 2, core, me + 1 - 2 * core
+
+
+def piece(ref, owner, rows):
     per = DV // rows
-
-    def piece(ref, owner):
-        head = owner // per
-        return ref.at[head, pl.ds(pl.multiple_of(lax.rem(owner, per) * rows, rows), rows)]
-
-    def remote(src, dst, ssem, rsem, other):
-        return pltpu.make_async_remote_copy(
-            src_ref=src,
-            dst_ref=dst,
-            send_sem=ssem,
-            recv_sem=rsem,
-            device_id={"seq": other},
-            device_id_type=MESH,
-        )
-
-    def arrived(ref, sem):
-        pltpu.make_async_copy(ref, ref, sem).wait()
-
-    own_b = pltpu.make_async_copy(piece(b_ref, me), bbuf.at[me], b_sem.at[me])
-    own_b.start()
-    if not backward:
-        own_a = pltpu.make_async_copy(a_ref.at[me // per], all_ref.at[me], a_sem.at[me])
-        own_a.start()
-    greet(count, me)
-
-    def deal(s, carry):
-        other = lax.rem(me + s, count)
-        if not backward:
-            remote(
-                a_ref.at[other // per], all_ref.at[me], asend_sem.at[other], a_sem.at[me], other
-            ).start()
-        remote(
-            piece(b_ref, other), bbuf.at[me], send_sem.at[other], b_sem.at[me], other
-        ).start()
-        return carry
-
-    lax.fori_loop(1, count, deal, 0)
-
-    sbuf[0] = jnp.zeros((rows, DK), F32)
-
-    def turn(t, carry):
-        j = count - 1 - t if backward else t
-
-        @pl.when(j == me)
+    return ref.at[owner // per, pl.ds(pl.multiple_of(lax.rem(owner, per) * rows, rows), rows)]
+
+
+def deliver(chips, chip, core, rows, sbuf, gin, send_sem, in_sem, slots):
+    for slot, j in slots:
+
+        @pl.when(chip == j)
         def _():
-            pltpu.make_async_copy(sbuf.at[t], piece(s_ref, me), s_sem.at[me]).start()
-
-        @pl.when(j != me)
+            pltpu.make_async_copy(sbuf.at[slot], piece(gin, chip, rows), in_sem.at[chip]).start()
+
+        @pl.when(chip != j)
         def _():
             remote(
-                sbuf.at[t], piece(s_ref, me), send_sem.at[count + j], s_sem.at[me], j
+                sbuf.at[slot],
+                piece(gin, chip, rows),
+                send_sem.at[j],
+                in_sem.at[chip],
+                seq=2 * j + core,
             ).start()
 
-        arrived(bbuf.at[j], b_sem.at[j])
-        if not backward:
-            arrived(all_ref.at[j], a_sem.at[j])
-        form = NN if backward else NT
-        sbuf[t + 1] = dot3(split(sbuf[t]), split(all_ref[j]), form) + bbuf[j]
+
+def forward_kernel(count, *refs):
+    (
+        a_ref, b_ref, s_ref, ah_ref, al_ref, first_ref, second_ref,
+        siba, sibb, comb, combb, firstb, abuf, bbuf, sbuf, gin, stage,
+        pair_a, pair_b, pair_as, pair_bs, deal_a, deal_b, in_a, in_b, send_sem, in_sem, fix_s, fix_r,
+    ) = refs
+    chips = count // 2
+    rows = OWN * DV // chips
+    me, chip, core, sibling = place(count)
+    mine, theirs = core * OWN, (1 - core) * OWN
+    greet(count, me, 2, ({"seq": sibling},))
+    for n in range(OWN):
+        remote(a_ref.at[theirs + n], siba.at[n], pair_as.at[n], pair_a.at[n], seq=sibling).start()
+        remote(b_ref.at[theirs + n], sibb.at[n], pair_bs.at[n], pair_b.at[n], seq=sibling).start()
+    lead = core == 0
+    per = DV // rows
+    for n in range(OWN):
+        arrived(siba.at[n], pair_a.at[n])
+        arrived(sibb.at[n], pair_b.at[n])
+        oa, ob, ta, tb = a_ref[mine + n], b_ref[mine + n], siba[n], sibb[n]
+        first, second = jnp.where(lead, oa, ta), jnp.where(lead, ta, oa)
+        fb, sb = jnp.where(lead, ob, tb), jnp.where(lead, tb, ob)
+        first_ref[n] = first
+        second_ref[n] = second
+        firstb[n] = fb
+        ss = split(second)
+        comb[n] = dot3(ss, split(first))
+        combb[n] = dot3(split(fb), ss, NT) + sb
+        for p in range(per):
+            owner = n * per + p
+
+            @pl.when(chip == owner)
+            def _():
+                pltpu.make_async_copy(comb.at[n], abuf.at[chip], in_a.at[chip]).start()
+                pltpu.make_async_copy(
+                    piece(combb, owner, rows), bbuf.at[chip], in_b.at[chip]
+                ).start()
+
+            @pl.when(chip != owner)
+            def _():
+                there = 2 * owner + core
+                remote(
+                    comb.at[n], abuf.at[chip], deal_a.at[owner], in_a.at[chip], seq=there
+                ).start()
+                remote(
+                    piece(combb, owner, rows),
+                    bbuf.at[chip],
+                    deal_b.at[owner],
+                    in_b.at[chip],
+                    seq=there,
+                ).start()
+
+    def take(j, carry):
+        arrived(abuf.at[j], in_a.at[j])
+        high, low = split(abuf[j])
+        ah_ref[j] = high
+        al_ref[j] = low
+        arrived(bbuf.at[j], in_b.at[j])
         return carry
 
-    lax.fori_loop(0, count, turn, 0)
+    lax.fori_loop(0, chips, take, 0)
+    state = jnp.zeros((rows, DK), F32)
+    batch = max(1, chips // 2)
+    for start in range(0, chips, batch):
+        for j in range(start, start + batch):
+            sbuf[j] = state
+            state = dot3(split(state), (ah_ref[j], al_ref[j]), NT) + bbuf[j]
+        deliver(
+            chips, chip, core, rows, sbuf, gin, send_sem, in_sem,
+            [(j, j) for j in range(start, start + batch)],
+        )
+
+    for n in range(OWN):
+        for p in range(per):
+            arrived(piece(gin, n * per + p, rows), in_sem.at[n * per + p])
+        entering = gin[n]
+        between = dot3(split(entering), split(first_ref[n]), NT) + firstb[n]
+        s_ref[mine + n] = jnp.where(lead, entering, between)
+        stage[n] = jnp.where(lead, between, entering)
+        remote(stage.at[n], s_ref.at[mine + n], fix_s.at[n], fix_r.at[n], seq=sibling).start()
+    for n in range(OWN):
+        arrived(siba.at[n], pair_as.at[n])
+        arrived(sibb.at[n], pair_bs.at[n])
+        arrived(stage.at[n], fix_s.at[n])
+        arrived(s_ref.at[theirs + n], fix_r.at[n])
 
     def settle(s, carry):
-        other = lax.rem(me + s, count)
-        arrived(piece(b_ref, other), send_sem.at[other])
-        arrived(sbuf.at[other], send_sem.at[count + other])
-        if not backward:
-            arrived(a_ref.at[other // per], asend_sem.at[other])
-        arrived(piece(s_ref, other), s_sem.at[other])
+        other = lax.rem(chip + s, chips)
+        arrived(abuf.at[other], deal_a.at[other])
+        arrived(bbuf.at[other], deal_b.at[other])
+        arrived(sbuf.at[other], send_sem.at[other])
         return carry
 
-    lax.fori_loop(1, count, settle, 0)
-    arrived(piece(s_ref, me), s_sem.at[me])
+    lax.fori_loop(1, chips, settle, 0)
+
+
+def backward_kernel(count, heads, blocks, *refs):
+    (
+        c_ref, ah_ref, al_ref, first_ref, second_ref, red_ref, s_ref, fin_ref,
+        sibc, combc, secondc, bbuf, sbuf, gin, stage, gather, zbuf,
+        pair_r, pair_s, deal_s, in_b, send_sem, in_sem, fix_s, fix_r,
+        red_s, red_r, z_s, z_r, fin_s, fin_r,
+    ) = refs
+    chips = count // 2
+    rows = OWN * DV // chips
+    me, chip, core, sibling = place(count)
+    mine, theirs = core * OWN, (1 - core) * OWN
+    line = lax.axis_index("head")
+    share = -(-blocks // count)
+    owners = -(-blocks // share)
+    peers = [lax.rem(line + s, heads) for s in range(1, heads)]
+    greet(count, me, 1, tuple({"head": peer} for peer in peers))
+    for n in range(OWN):
+        remote(c_ref.at[theirs + n], sibc.at[n], pair_s.at[n], pair_r.at[n], seq=sibling).start()
+
+    def scatter(o, carry):
+        @pl.when(o != me)
+        def _():
+            remote(
+                red_ref.at[pl.ds(o * share, share)],
+                gather.at[me],
+                red_s.at[o],
+                red_r.at[me],
+                seq=o,
+            ).start()
+
+        return carry
+
+    lead = core == 0
+    per = DV // rows
+    for n in range(OWN):
+        arrived(sibc.at[n], pair_r.at[n])
+        oc, tc = c_ref[mine + n], sibc[n]
+        first, second = jnp.where(lead, oc, tc), jnp.where(lead, tc, oc)
+        secondc[n] = second
+        combc[n] = dot3(split(second), split(first_ref[n])) + first
+        for p in range(per):
+            owner = n * per + p
+
+            @pl.when(chip == owner)
+            def _():
+                pltpu.make_async_copy(
+                    piece(combc, owner, rows), bbuf.at[chip], in_b.at[chip]
+                ).start()
+
+            @pl.when(chip != owner)
+            def _():
+                remote(
+                    piece(combc, owner, rows),
+                    bbuf.at[chip],
+                    deal_s.at[owner],
+                    in_b.at[chip],
+                    seq=2 * owner + core,
+                ).start()
+
+    lax.fori_loop(0, owners, scatter, 0)
+
+    def take(j, carry):
+        arrived(bbuf.at[j], in_b.at[j])
+        return carry
+
+    lax.fori_loop(0, chips, take, 0)
+    state = jnp.zeros((rows, DK), F32)
+    batch = max(1, chips // 2)
+    for start in range(0, chips, batch):
+        for t in range(start, start + batch):
+            j = chips - 1 - t
+            sbuf[t] = state
+            state = dot3(split(state), (ah_ref[j], al_ref[j])) + bbuf[j]
+        deliver(
+            chips, chip, core, rows, sbuf, gin, send_sem, in_sem,
+            [(t, chips - 1 - t) for t in range(start, start + batch)],
+        )
+
+    @pl.when(me < owners)
+    def _():
+        gather[me] = red_ref[pl.ds(me * share, share)]
+
+        def add(s, total):
+            return total + gather[s]
+
+        def got(s, carry):
+            other = lax.rem(me + s, count)
+            arrived(gather.at[other], red_r.at[other])
+            return carry
+
+        lax.fori_loop(1, count, got, 0)
+        total = lax.fori_loop(0, count, add, jnp.zeros((share, RANK, 128), F32))
+        zbuf[line] = total
+        for peer in peers:
+            remote(zbuf.at[line], zbuf.at[line], z_s.at[peer], z_r.at[line], head=peer).start()
+
+    for n in range(OWN):
+        for p in range(per):
+            arrived(piece(gin, n * per + p, rows), in_sem.at[n * per + p])
+        leaving = gin[n]
+        between = dot3(split(leaving), split(second_ref[n])) + secondc[n]
+        s_ref[mine + n] = jnp.where(lead, between, leaving)
+        stage[n] = jnp.where(lead, leaving, between)
+        remote(stage.at[n], s_ref.at[mine + n], fix_s.at[n], fix_r.at[n], seq=sibling).start()
+
+    @pl.when(me < owners)
+    def _():
+        for peer in peers:
+            arrived(zbuf.at[peer], z_r.at[peer])
+        every = zbuf[0]
+        for z in range(1, heads):
+            every = every + zbuf[z]
+        block = me * share + lax.broadcasted_iota(jnp.int32, (share, RANK, 128), 0)
+        own = fin_ref.at[pl.ds(me * share, share)]
+        own[...] = jnp.where(block < HEADS, zbuf[line], every)
+
+        def tell(s, carry):
+            other = lax.rem(me + s, count)
+            remote(own, own, fin_s.at[other], fin_r.at[me], seq=other).start()
+            return carry
+
+        lax.fori_loop(1, count, tell, 0)
+
+    for n in range(OWN):
+        arrived(sibc.at[n], pair_s.at[n])
+        arrived(stage.at[n], fix_s.at[n])
+        arrived(s_ref.at[theirs + n], fix_r.at[n])
+
+    def settle(s, carry):
+        other = lax.rem(chip + s, chips)
+        arrived(bbuf.at[other], deal_s.at[other])
+        arrived(sbuf.at[other], send_sem.at[other])
+        return carry
+
+    lax.fori_loop(1, chips, settle, 0)
+
+    def heard(o, carry):
+        @pl.when(o != me)
+        def _():
+            arrived(gather.at[o], red_s.at[o])
+            arrived(fin_ref.at[pl.ds(o * share, share)], fin_r.at[o])
+
+        return carry
+
+    lax.fori_loop(0, owners, heard, 0)
+
+    @pl.when(me < owners)
+    def _():
+        for peer in peers:
+            arrived(zbuf.at[peer], z_s.at[peer])
+
+        def told(s, carry):
+            other = lax.rem(me + s, count)
+            arrived(fin_ref.at[pl.ds(me * share, share)], fin_s.at[other])
+            return carry
+
+        lax.fori_loop(1, count, told, 0)
 
 
 VM = pl.BlockSpec(memory_space=pltpu.VMEM)
@@ -446,22 +675,30 @@
     return jax.ShapeDtypeStruct(shape, dtype)
 
 
+DMA = pltpu.SemaphoreType.DMA
+
+
 def forward_scan(a, bt, count):
-    rows = HEADS * DV // count
+    chips = count // 2
+    rows = OWN * DV // chips
+    half = pltpu.VMEM((OWN, DK, DV), F32)
+    part = pltpu.VMEM((chips, rows, DK), F32)
     return pl.pallas_call(
-        functools.partial(scan_kernel, count, False),
-        out_shape=(struct(HEADS, DV, DK), struct(count, DK, DK)),
+        functools.partial(forward_kernel, count),
+        out_shape=(
+            struct(HEADS, DV, DK),
+            struct(chips, DK, DK, dtype=BF16),
+            struct(chips, DK, DK, dtype=BF16),
+            struct(OWN, DK, DK),
+            struct(OWN, DK, DK),
+        ),
         in_specs=[VM] * 2,
-        out_specs=(VM, VM),
-        scratch_shapes=[
-            pltpu.VMEM((count, rows, DK), F32),
-            pltpu.VMEM((count + 1, rows, DK), F32),
-            pltpu.SemaphoreType.DMA((2 * count,)),
-            pltpu.SemaphoreType.DMA((count,)),
-            pltpu.SemaphoreType.DMA((count,)),
-            pltpu.SemaphoreType.DMA((count,)),
-            pltpu.SemaphoreType.DMA((count,)),
-        ],
+        out_specs=(VM,) * 5,
+        scratch_shapes=[half] * 5
+        + [pltpu.VMEM((chips, DK, DK), F32), part, part, half, half]
+        + [DMA((OWN,))] * 4
+        + [DMA((chips,))] * 6
+        + [DMA((OWN,))] * 2,
         compiler_params=pltpu.CompilerParams(
             collective_id=0, has_side_effects=True, vmem_limit_bytes=LIMIT
         ),
@@ -469,25 +706,35 @@
     )(a, bt)
 
 
-def backward_scan(ct, everyone, count):
-    rows = HEADS * DV // count
+def backward_scan(ct, high, low, first, second, red, count, heads):
+    chips = count // 2
+    rows = OWN * DV // chips
+    half = pltpu.VMEM((OWN, DK, DV), F32)
+    part = pltpu.VMEM((chips, rows, DK), F32)
+    blocks = red.shape[0]
+    share = -(-blocks // count)
     return pl.pallas_call(
-        functools.partial(scan_kernel, count, True),
-        out_shape=struct(HEADS, DV, DK),
-        in_specs=[VM] * 2,
-        out_specs=VM,
-        scratch_shapes=[
-            pltpu.VMEM((count, rows, DK), F32),
-            pltpu.VMEM((count + 1, rows, DK), F32),
-            pltpu.SemaphoreType.DMA((2 * count,)),
-            pltpu.SemaphoreType.DMA((count,)),
-            pltpu.SemaphoreType.DMA((count,)),
-        ],
+        functools.partial(backward_kernel, count, heads, blocks),
+        out_shape=(struct(HEADS, DV, DK), struct(*red.shape)),
+        in_specs=[VM] * 6,
+        out_specs=(VM, VM),
+        scratch_shapes=[half] * 3
+        + [part, part, half, half]
+        + [
+            pltpu.VMEM((count, share, RANK, 128), F32),
+            pltpu.VMEM((heads, share, RANK, 128), F32),
+        ]
+        + [DMA((OWN,))] * 2
+        + [DMA((chips,))] * 4
+        + [DMA((OWN,))] * 2
+        + [DMA((count,))] * 2
+        + [DMA((heads,))] * 2
+        + [DMA((count,))] * 2,
         compiler_params=pltpu.CompilerParams(
             collective_id=1, has_side_effects=True, vmem_limit_bytes=LIMIT
         ),
         name="state_gradients",
-    )(ct, everyone)
+    )(ct, high, low, first, second, red)
 
 
 def body(
@@ -504,6 +751,7 @@
     output_gradient,
 ):
     count = lax.axis_size("seq")
+    blocks = HEADS + output_gradient.shape[1] // 128
     params = pltpu.CompilerParams(vmem_limit_bytes=LIMIT)
     per_head = struct(HEADS, TOK, DK)
     a, bt, w, u, e, o, zt, yh, yl, gn, gr, rows, cols = pl.pallas_call(
@@ -546,8 +794,8 @@
         adapter_lowering,
         adapter_raising,
     )
-    s0, everyone = forward_scan(a, bt, count)
-    ct, xt, uf, ft, dq, down, lift = pl.pallas_call(
+    s0, high, low, first, second = forward_scan(a, bt, count)
+    ct, xt, uf, ft, dq, red = pl.pallas_call(
         middle_kernel,
         out_shape=(
             struct(HEADS, DV, DK),
@@ -555,11 +803,10 @@
             per_head,
             struct(HEADS, DK, TOK),
             struct(TOK, KEYS * DK),
-            struct(RANK, HEADS * DV),
-            struct(RANK, output_gradient.shape[1]),
+            struct(blocks, RANK, 128),
         ),
         in_specs=[SM] + [VM] * 16,
-        out_specs=(VM,) * 7,
+        out_specs=(VM,) * 6,
         scratch_shapes=[
             pltpu.VMEM((KEYS, TOK, DK), BF16),
             pltpu.VMEM((KEYS, TOK, DK), BF16),
@@ -587,18 +834,20 @@
         output_gradient,
         adapter_lowering,
     )
-    grad_down = lax.psum(down, "seq")
-    raising_gradient = lax.psum(lift, ("seq", "head"))
-    ds = backward_scan(ct, everyone, count)
-    dk, dv, db = pl.pallas_call(
+    ds, fin = backward_scan(
+        ct, high, low, first, second, red, count, lax.axis_size("head")
+    )
+    dk, dv, db, grad_down, raising_gradient = pl.pallas_call(
         last_kernel,
         out_shape=(
             struct(TOK, KEYS * DK),
             struct(TOK, HEADS * DV),
             struct(HEADS, TOK),
+            struct(RANK, HEADS * DV),
+            struct(RANK, output_gradient.shape[1]),
         ),
-        in_specs=[SM] + [VM] * 9,
-        out_specs=(VM,) * 3,
+        in_specs=[SM] + [VM] * 10,
+        out_specs=(VM,) * 5,
         scratch_shapes=[
             pltpu.VMEM((KEYS, TOK, DK), BF16),
             pltpu.VMEM((KEYS, DK, TOK), BF16),
@@ -607,7 +856,7 @@
         ],
         compiler_params=params,
         name="last_pass",
-    )(value_to_key_head, ds, s0, key_matrix_rows, xt, zt, uf, ft, rows, cols)
+    )(value_to_key_head, ds, s0, key_matrix_rows, xt, zt, uf, ft, rows, cols, fin)
     return (dq, dk, dv, db, grad_down, raising_gradient)
 
 

time: 361 us -> 122 us (0.34)
  waiting for transfers between devices: 212 us -> 0 us
  between operations: 14.1 us -> 0.65 us
  Pallas kernels: 132 us -> 121 us
    psum x2 -> x0, waiting for transfers between devices: 211 us -> none  [the longest x1 144 us: body(): raising_gradient = lax.psum(lift, ('seq', 'head'))]
    pallas_call x2, Pallas kernels: 87.4 us -> 76.6 us  [the longest x1 46 us: forward_scan(): pl.pallas_call(functools.partial(forward_kernel, count), out_shape=(struc...]
  transfers between devices with their start and end apart: 2 -> 0, of which waited for: 2 -> 0; matrix products, arithmetic and copies ran while one was open for 0% -> 0% of each run, Pallas kernels for 11% -> 0%
where the time goes in v2:
time: 122 us; the launch traced here: 121 us
  Pallas kernels  121 us (99%)
    pallas_call x1, Pallas kernels, forward_scan(): pl.pallas_call(functools.partial(forward_kernel, count), out_shape=(struc...  46 us
    pallas_call x1, Pallas kernels, backward_scan(): pl.pallas_call(functools.partial(backward_kernel, count, heads, blocks),...  30.6 us
    pallas_call x1, Pallas kernels, body(): pl.pallas_call(local_kernel, out_shape=(struct(HEADS, DK, DK), struct(HEA...  21.1 us
    pallas_call x1, Pallas kernels, body(): pl.pallas_call(middle_kernel, out_shape=(struct(HEADS, DV, DK), struct(HE...  13.1 us
    pallas_call x1, Pallas kernels, body(): pl.pallas_call(last_kernel, out_shape=(struct(TOK, KEYS * DK), struct(TOK...  10 us

profile of v2, /device:TPU:1, one launch (start us, length us, event | category | flops | bytes accessed | tf_op | source)
XLA Modules:
  0.0 121.4 jit_solution(14443805607940325439)
XLA Ops:
  0.6 21.1 %local_pass.1 = (f32[8,128,128]{2,1,0:T(8,128)}, f32[8,128,128]{2,1,0:T(8,128)}, f32[8,256,128]{2,1,0:T(8,128)}, f32[8,256,128]{2,1,0:T(8,128)}, f32[8,256,128]{...) custom-call(s32[8]{0:T(128)} %which.5, ...), custom_call_target="tpu_custom_call" | custom-call | tf_op jit(solution)/shard_map/local_pass/pallas_call | solution.py:757
  21.7 46.0 %forward_states.1 = (f32[8,128,128]{2,1,0:T(8,128)}, bf16[16,128,128]{2,1,0:T(8,128)(2,1)}, bf16[16,128,128]{2,1,0:T(8,128)(2,1)}, f32[4,128,128]{2,1,0:T(8,128)}, f32[4,128,128]{2,1,0:T(8,128)}) custom-call(f32[8,128,128]{2,1,0:T(8,128)} %get-tuple-element.37.refs_0_, f32[8,128,128]{2,1,0:T(8,128)} %get-tuple-element.38.refs_1_), custom_call_target="tpu_custom_call" | custom-call | tf_op jit(solution)/shard_map/forward_states/pallas_call | solution.py:686
  67.7 13.1 %middle_pass.1 = (f32[8,128,128]{2,1,0:T(8,128)}, f32[8,128,256]{2,1,0:T(8,128)}, f32[8,256,128]{2,1,0:T(8,128)}, f32[8,128,256]{2,1,0:T(8,128)}, f32[256,512]{1,0:T(8,128)}, /*index=5*/f32[24,16,128]{2,1,0:T(8,128)}) custom-call(s32[8]{0:T(128)} %which.5, f32[8,128,128]{2,1,0:T(8,128)} %get-tuple-element.39.s0_ref, bf16[256,512]{1,0:T(8,128)(2,1)} %q_ref.3, ...), custom_call_target="tpu_custom_call" | custom-call | tf_op jit(solution)/shard_map/middle_pass/pallas_call | solution.py:798
  80.8 30.6 %state_gradients.1 = (f32[8,128,128]{2,1,0:T(8,128)}, f32[24,16,128]{2,1,0:T(8,128)}) custom-call(f32[8,128,128]{2,1,0:T(8,128)} %get-tuple-element.51.refs_0_, bf16[16,128,128]{2,1,0:T(8,128)(2,1)} %get-tuple-element.52.refs_1_, bf16[16,128,128]{2,1,0:T(8,128)(2,1)} %get-tuple-element.53.refs_2_, f32[4,128,128]{2,1,0:T(8,128)} %get-tuple-element.54.refs_3_, ...), custom_call_target="tpu_custom_call" | custom-call | tf_op jit(solution)/shard_map/state_gradients/pallas_call | solution.py:716
  111.4 10.0 %last_pass.1 = (f32[256,512]{1,0:T(8,128)}, f32[256,1024]{1,0:T(8,128)}, f32[8,256]{1,0:T(8,128)}, f32[16,1024]{1,0:T(8,128)}, f32[16,2048]{1,0:T(8,128)}) custom-call(s32[8]{0:T(128)} %which.5, f32[8,128,128]{2,1,0:T(8,128)} %get-tuple-element.57.ds_ref, f32[8,128,128]{2,1,0:T(8,128)} %get-tuple-element.39.s0_ref, bf16[256,512]{1,0:T(8,128)(2,1)} %k_ref.5, ...), custom_call_target="tpu_custom_call" | custom-call | tf_op jit(solution)/shard_map/last_pass/pallas_call | solution.py:840

commit v3 on v0

v3 whole, which is shorter than its diff:
```python
import functools
import types

import jax
import jax.numpy as jnp
from jax import lax
from jax.experimental import pallas as pl
from jax.experimental.pallas import tpu as pltpu
from jax.sharding import PartitionSpec as P

DK = 128
DV = 128
TOK = 256
HALF = 128
HEADS = 8
KEYS = 4
RANK = 16
EPS = 1e-06
F32 = jnp.float32
BF16 = jnp.bfloat16
MESH = pl.DeviceIdType.MESH

NN = (((1,), (0,)), ((), ()))
NT = (((1,), (1,)), ((), ()))
TN = (((0,), (0,)), ((), ()))


def dot(x, y, form=NN):
    return lax.dot_general(x, y, form, preferred_element_type=F32)


def split(x):
    high = x.astype(BF16)
    return high, (x - high.astype(F32)).astype(BF16)


def cat(parts, axis):
    return jnp.concatenate(parts, axis=axis)


def dot3(x, y, form=NN):
    cx, cy = form[0][0][0], form[0][1][0]
    return dot(cat([x[0], x[1], x[0]], cx), cat([y[0], y[0], y[1]], cy), form)


def dot2(x, exact, form=NN):
    cx, cy = form[0][0][0], form[0][1][0]
    return dot(cat(list(x), cx), cat([exact, exact], cy), form)


def dot2r(exact, y, form=NN):
    cx, cy = form[0][0][0], form[0][1][0]
    return dot(cat([exact, exact], cx), cat(list(y), cy), form)


def square(x, y):
    right = cat([cat([y[0], y[1]], 1), cat([y[0], jnp.zeros_like(y[1])], 1)], 0)
    both = dot(cat([x[0], x[1]], 1), right)
    return both[:, :HALF] + both[:, HALF:]


def grid_of(rows, columns):
    return (
        lax.broadcasted_iota(jnp.int32, (rows, columns), 0),
        lax.broadcasted_iota(jnp.int32, (rows, columns), 1),
    )


def inverses(blocks):
    row, col = grid_of(HALF, HALF)
    eye = jnp.where(row == col, 1.0, 0.0).astype(F32)
    pairs = ((row >> 1) == (col >> 1)) & (row > col)
    found = [eye - jnp.where(pairs, block, 0.0) for block in blocks]
    for level in range(1, 7):
        here = ((row >> (level + 1)) == (col >> (level + 1))) & ((row >> level) > (col >> level))
        halves = [split(x) for x in found]
        inner = [
            split(square(split(jnp.where(here, block, 0.0)), x))
            for block, x in zip(blocks, halves)
        ]
        found = [x - square(h, y) for x, h, y in zip(found, halves, inner)]
    return found


ROW_R, ROW_C, ROW_P, ROW_G, ROW_BG, ROW_AG, ROW_KEY = 0, 8, 16, 24, 32, 40, 48


def last_kernel(
    which,
    ds_ref,
    s0_ref,
    k_ref,
    xt_ref,
    zt_ref,
    u_ref,
    ft_ref,
    rows_ref,
    cols_ref,
    fin_ref,
    dqin_ref,
    dq_ref,
    dk_ref,
    dv_ref,
    db_ref,
    down_ref,
    raise_ref,
    k4,
    kt4,
    acc4,
    acct4,
):
    for m in range(KEYS):
        at = slice(m * DK, (m + 1) * DK)
        k4[m] = k_ref[:, at]
        kt4[m] = k_ref[:, at].T
    acc4[...] = jnp.zeros_like(acc4)
    acct4[...] = jnp.zeros_like(acct4)
    dq_ref[...] = dqin_ref[...]
    for n in range(HEADS):
        down_ref[:, n * 128 : (n + 1) * 128] = fin_ref[n]
    for n in range(raise_ref.shape[1] // 128):
        raise_ref[:, n * 128 : (n + 1) * 128] = fin_ref[HEADS + n]
    row, col = grid_of(TOK, TOK)
    for h in range(HEADS):
        m = which[h] % KEYS
        dst = ds_ref[h]
        drt = xt_ref[h] + dot3(split(dst), split(zt_ref[h]))
        dr = drt.T
        dv_ref[:, h * DV : (h + 1) * DV] = dr
        drs, us = split(dr), split(u_ref[h])
        dl = split(jnp.where(row > col, -dot3(drs, us, NT), 0.0))
        kt = kt4[m].astype(F32)
        rk = split(kt * rows_ref[ROW_R + h : ROW_R + h + 1, :])
        ck = split(k4[m].astype(F32) * cols_ref[:, ROW_C + h : ROW_C + h + 1])
        last = rows_ref[ROW_G + h : ROW_G + h + 1, TOK - 1 : TOK]
        f = ft_ref[h] + dot3(rk, dl) + last * dot3(split(dst.T), us, NT)
        db_ref[h : h + 1, :] = (
            jnp.sum(kt * f, axis=0, keepdims=True) * rows_ref[ROW_AG + h : ROW_AG + h + 1, :]
        )
        own = dot3(dl, ck) - dot3(drs, split(s0_ref[h]))
        acc4[m] = acc4[m] + own * cols_ref[:, ROW_G + h : ROW_G + h + 1]
        acct4[m] = acct4[m] + f * rows_ref[ROW_BG + h : ROW_BG + h + 1, :]
    for m in range(KEYS):
        total = acc4[m] + acct4[m].T
        k = k4[m].astype(F32)
        inv = cols_ref[:, ROW_KEY + m : ROW_KEY + m + 1]
        along = jnp.sum(total * k, axis=-1, keepdims=True)
        dk_ref[:, m * DK : (m + 1) * DK] = inv * (total - k * (inv * inv * along))


def remote(src, dst, ssem, rsem, **where):
    return pltpu.make_async_remote_copy(
        src_ref=src,
        dst_ref=dst,
        send_sem=ssem,
        recv_sem=rsem,
        device_id=where,
        device_id_type=MESH,
    )


def arrived(ref, sem):
    pltpu.make_async_copy(ref, ref, sem).wait()


OWN = HEADS // 2


def place(count):
    me = lax.axis_index("seq")
    core = lax.rem(me, 2)
    return me, me // 2, core, me + 1 - 2 * core


def piece(ref, owner, rows):
    per = DV // rows
    return ref.at[owner // per, pl.ds(pl.multiple_of(lax.rem(owner, per) * rows, rows), rows)]


def turns(chip, chips, act):
    def one(s, carry):
        act(lax.rem(chip + s, chips))
        return carry

    lax.fori_loop(0, chips, one, 0)


def deliver(chips, chip, core, rows, sbuf, into, send_sem, in_sem):
    mine = chip - core * (chips // 2)

    def act(j):
        @pl.when(chip == j)
        def _():
            pltpu.make_async_copy(sbuf.at[j], piece(into, mine, rows), in_sem.at[mine]).start()

        @pl.when(chip != j)
        def _():
            remote(
                sbuf.at[j],
                piece(into, mine, rows),
                send_sem.at[j],
                in_sem.at[mine],
                seq=2 * j + core,
            ).start()

    turns(chip, chips, act)


def table(r):
    lane = lax.broadcasted_iota(jnp.int32, (HEADS, TOK), 1)
    gamma = 1.0 - r.code[...].astype(F32) * 2.0 ** (-20)
    step = 1
    while step < TOK:
        gamma = gamma * jnp.where(lane >= step, pltpu.roll(gamma, step, 1), 1.0)
        step *= 2
    back = 1.0 / gamma
    ones = jnp.ones((8, DK), BF16)
    r.rows[...] = jnp.zeros_like(r.rows)
    for m in range(KEYS):
        at = slice(m * DK, (m + 1) * DK)
        k = r.k[:, at]
        q = r.q[:, at]
        r.k4[m] = k
        r.q4[m] = q
        r.kt4[m] = k.T
        r.qt4[m] = q.T
        r.kk4[m] = dot(k, k, NT)
        r.qk4[m] = dot(q, k, NT)
        kf, qf = k.astype(F32), q.astype(F32)
        ksum = dot2r(ones, split(kf * kf), NT)[0:1]
        qsum = dot2r(ones, split(qf * qf), NT)[0:1]
        r.rows[ROW_KEY + m : ROW_KEY + m + 1, :] = lax.rsqrt(ksum + EPS)
        r.rows[ROW_KEY + KEYS + m : ROW_KEY + KEYS + m + 1, :] = lax.rsqrt(qsum + EPS)
    rate = r.rate[...]
    for h in range(HEADS):
        m = r.which[h] % KEYS
        a = r.rows[pl.ds(ROW_KEY + m, 1), :]
        b = r.rows[pl.ds(ROW_KEY + KEYS + m, 1), :] * DK ** (-0.5)
        g, i, w = gamma[h : h + 1], back[h : h + 1], rate[h : h + 1]
        for at, value in (
            (ROW_R, g * a),
            (ROW_C, a * w * i),
            (ROW_P, g * b),
            (ROW_G, g),
            (ROW_BG, w * i),
            (ROW_AG, a * i),
        ):
            r.rows[at + h : at + h + 1, :] = value
    r.cols[...] = r.rows[...].T


def column(r, at):
    return r.cols[:, at : at + 1]


def line_of(r, at):
    return r.rows[at : at + 1, :]


def summaries(r, heads):
    row, col = grid_of(TOK, TOK)
    srow, scol = grid_of(HALF, HALF)
    eye = jnp.where(srow == scol, 1.0, 0.0).astype(F32)
    blocks, corners = [], []
    for h in heads:
        m = r.which[h] % KEYS
        strict = jnp.where(
            row > col, r.kk4[m] * column(r, ROW_R + h) * line_of(r, ROW_C + h), 0.0
        )
        blocks += [strict[:HALF, :HALF], strict[HALF:, HALF:]]
        corners.append(split(strict[HALF:, :HALF]))
    found = inverses(blocks)
    for n, h in enumerate(heads):
        m = r.which[h] % KEYS
        first, second = split(found[2 * n]), split(found[2 * n + 1])
        corner = split(-square(second, split(square(corners[n], first))))
        blank = jnp.zeros((HALF, HALF), BF16)
        t = tuple(
            cat([cat([first[i], blank], 1), cat([corner[i], second[i]], 1)], 0) for i in range(2)
        )
        r.th[h] = t[0]
        r.tl[h] = t[1]
        final = r.rows[ROW_G + h : ROW_G + h + 1, TOK - 1 : TOK]
        ended = split(r.kt4[m].astype(F32) * (line_of(r, ROW_C + h) * final))
        zt = dot3(ended, t)
        zs = split(zt)
        r.zt[h] = zt
        g = split(r.k4[m].astype(F32) * column(r, ROW_R + h))
        r.a[h] = final * eye - dot3(zs, g)
        r.b[h] = dot2r(r.v[:, h * DV : (h + 1) * DV].T, zs, NT)


def readings(r):
    row, col = grid_of(TOK, TOK)
    for h in range(HEADS):
        m = r.which[h] % KEYS
        t = (r.th[h], r.tl[h])
        q = r.q4[m].astype(F32)
        g = split(r.k4[m].astype(F32) * column(r, ROW_R + h))
        pair = cat([g[0], r.v[:, h * DV : (h + 1) * DV]], 1)
        wu = dot2(t, pair)
        r.w[h] = wu[:, :DK] + dot(t[0], g[1])
        r.u[h] = wu[:, DK:]
        mixing = jnp.where(
            row >= col, r.qk4[m] * column(r, ROW_P + h) * line_of(r, ROW_C + h), 0.0
        )
        y = split(dot3(split(mixing), t))
        r.yh[h] = y[0]
        r.yl[h] = y[1]
        eo = dot2(y, pair)
        r.e[h] = q * column(r, ROW_P + h) - (eo[:, :DK] + dot(y[0], g[1]))
        r.o[h] = eo[:, DK:]


def projections(r):
    rs = split(r.lift[...])
    both = dot(cat(list(rs), 0), r.og[...], NT)
    grt = both[:RANK] + both[RANK:]
    gs = split(2.0 * grt)
    r.grh[...] = gs[0]
    r.grl[...] = gs[1]
    for h in range(HEADS):
        at = slice(h * DV, (h + 1) * DV)
        low = dot3(gs, split(r.lower[:, at]), TN)
        r.gn[:, at] = dot(r.og[...], r.weight[at, :], NT) + low


def outputs(r, heads):
    gain = r.gain[...]
    for h in heads:
        es = split(r.e[h])
        o = r.o[h] + dot3(es, split(r.s0[h]), NT)
        scale = lax.rsqrt(jnp.mean(o * o, axis=-1, keepdims=True) + EPS)
        gn = r.gn[:, h * DV : (h + 1) * DV] * gain
        tail = jnp.mean(gn * o, axis=-1, keepdims=True)
        do = scale * gn - o * (scale * scale * scale * tail)
        normed = split(o * scale * gain)
        r.nh[h] = normed[0]
        r.nl[h] = normed[1]
        r.do[h] = do
        dts = split(do.T)
        r.dth[h] = dts[0]
        r.dtl[h] = dts[1]
        r.ct[h] = dot3(dts, es)


def adapters(r):
    gs = (r.grh[...], r.grl[...])
    rank = jnp.zeros((RANK, TOK), F32)
    for h in range(HEADS):
        normed = (r.nh[h], r.nl[h])
        rank = rank + dot3(split(r.lower[:, h * DV : (h + 1) * DV]), normed, NT)
        r.red[h] = dot3(gs, normed)
    lift = 2.0 * dot2(split(rank), r.og[...])
    for n in range(lift.shape[1] // 128):
        r.red[HEADS + n] = lift[:, n * 128 : (n + 1) * 128]


def mixtures(r):
    row, col = grid_of(TOK, TOK)
    for h in range(HEADS):
        m = r.which[h] % KEYS
        ss = split(r.s0[h])
        u = r.u[h] - dot3(split(r.w[h]), ss, NT)
        r.uf[h] = u
        r.xt[h] = dot3((r.dth[h], r.dtl[h]), (r.yh[h], r.yl[h]))
        ds, us = split(r.do[h]), split(u)
        dp = split(jnp.where(row >= col, dot3(ds, us, NT), 0.0))
        ck = split(r.k4[m].astype(F32) * column(r, ROW_C + h))
        r.dqh[h] = (dot3(ds, ss) + dot3(dp, ck)) * column(r, ROW_G + h)
        pq = split(r.qt4[m].astype(F32) * line_of(r, ROW_P + h))
        r.ft[h] = dot3(pq, dp)
    for m in range(KEYS):
        one, two = 0, 0
        for h in range(HEADS):
            two = jnp.where(r.which[h] % KEYS == m, h, two)
            one = jnp.where(r.which[HEADS - 1 - h] % KEYS == m, HEADS - 1 - h, one)
        total = r.dqh[one] + r.dqh[two]
        q = r.q4[m].astype(F32)
        inv = column(r, ROW_KEY + KEYS + m)
        along = jnp.sum(total * q, axis=-1, keepdims=True)
        r.dq[:, m * DK : (m + 1) * DK] = (DK ** (-0.5) * inv) * (total - q * (inv * inv * along))


def main_kernel(count, lines, blocks, names, *refs):
    r = types.SimpleNamespace(**dict(zip(names, refs)))
    chips = count // 2
    owners = chips // 2
    rows = OWN * DV // owners
    per = DV // rows
    me, chip, core, sibling = place(count)
    mine, theirs = core * OWN, (1 - core) * OWN
    lead = core == 0
    holding = chip // owners == core
    line = lax.axis_index("head")
    share = -(-blocks // chips)
    holders = blocks // share
    summing = jnp.logical_and(chip // owners != core, chip < holders)
    peers = [lax.rem(line + s, lines) for s in range(1, lines)]
    barrier = pltpu.get_barrier_semaphore()

    def hello(s, carry):
        other = lax.rem(me + s, count)
        pl.semaphore_signal(barrier, inc=1, device_id={"seq": other}, device_id_type=MESH)
        return carry

    lax.fori_loop(1, count, hello, 0)
    for peer in peers:
        pl.semaphore_signal(barrier, inc=1, device_id={"head": peer}, device_id_type=MESH)

    table(r)
    for half in range(2):
        summaries(r, range(half * OWN, (half + 1) * OWN))
        if half == 0:
            pl.semaphore_wait(barrier, count - 1 + len(peers))

        @pl.when(core != half)
        def _():
            for n in range(OWN):
                h = half * OWN + n
                remote(
                    r.a.at[h], r.siba.at[n], r.pair_as.at[n], r.pair_a.at[n], seq=sibling
                ).start()
                remote(
                    r.b.at[h], r.sibb.at[n], r.pair_bs.at[n], r.pair_b.at[n], seq=sibling
                ).start()

    for n in range(OWN):
        arrived(r.siba.at[n], r.pair_a.at[n])
        arrived(r.sibb.at[n], r.pair_b.at[n])
    for n in range(OWN):
        oa, ob, ta, tb = r.a[mine + n], r.b[mine + n], r.siba[n], r.sibb[n]
        first, second = jnp.where(lead, oa, ta), jnp.where(lead, ta, oa)
        fb, sb = jnp.where(lead, ob, tb), jnp.where(lead, tb, ob)
        r.first[n] = first
        r.second[n] = second
        r.firstb[n] = fb
        ss = split(second)
        r.comb[n] = dot3(ss, split(first))
        r.combb[n] = dot3(split(fb), ss, NT) + sb

    def deal(w):
        there = core * owners + w

        @pl.when(chip == there)
        def _():
            pltpu.make_async_copy(r.comb.at[w // per], r.abuf.at[chip], r.in_a.at[chip]).start()
            pltpu.make_async_copy(
                piece(r.combb, w, rows), r.bbuf.at[chip], r.in_b.at[chip]
            ).start()

        @pl.when(chip != there)
        def _():
            device = 2 * there + core
            remote(
                r.comb.at[w // per], r.abuf.at[chip], r.deal_a.at[w], r.in_a.at[chip], seq=device
            ).start()
            remote(
                piece(r.combb, w, rows),
                r.bbuf.at[chip],
                r.deal_b.at[w],
                r.in_b.at[chip],
                seq=device,
            ).start()

    turns(lax.rem(chip, owners), owners, deal)
    readings(r)
    projections(r)

    @pl.when(holding)
    def _():
        def take(j, carry):
            arrived(r.abuf.at[j], r.in_a.at[j])
            high, low = split(r.abuf[j])
            r.ah[j] = high
            r.al[j] = low
            arrived(r.bbuf.at[j], r.in_b.at[j])
            return carry

        lax.fori_loop(0, chips, take, 0)
        state = jnp.zeros((rows, DK), F32)
        for j in range(chips):
            r.sbuf[j] = state
            state = dot3(split(state), (r.ah[j], r.al[j]), NT) + r.bbuf[j]
        deliver(chips, chip, core, rows, r.sbuf, r.gin, r.send, r.in_s)

    for w in range(owners):
        arrived(piece(r.gin, w, rows), r.in_s.at[w])
    for n in range(OWN):
        entering = r.gin[n]
        between = dot3(split(entering), split(r.first[n]), NT) + r.firstb[n]
        r.s0[mine + n] = jnp.where(lead, entering, between)
        r.stage[n] = jnp.where(lead, between, entering)
    for n in range(OWN):
        remote(
            r.stage.at[n], r.s0.at[mine + n], r.fix_s.at[n], r.fix_r.at[n], seq=sibling
        ).start()
    for n in range(OWN):
        arrived(r.s0.at[theirs + n], r.fix_r.at[n])

    for half in range(2):
        outputs(r, range(half * OWN, (half + 1) * OWN))

        @pl.when(core != half)
        def _():
            for n in range(OWN):
                remote(
                    r.ct.at[half * OWN + n],
                    r.sibc.at[n],
                    r.pair_cs.at[n],
                    r.pair_c.at[n],
                    seq=sibling,
                ).start()

    for n in range(OWN):
        arrived(r.sibc.at[n], r.pair_c.at[n])
    for n in range(OWN):
        oc, tc = r.ct[mine + n], r.sibc[n]
        first, second = jnp.where(lead, oc, tc), jnp.where(lead, tc, oc)
        r.secondc[n] = second
        r.combc[n] = dot3(split(second), split(r.first[n])) + first

    def deal_back(w):
        there = core * owners + w

        @pl.when(chip == there)
        def _():
            pltpu.make_async_copy(
                piece(r.combc, w, rows), r.cbuf.at[chip], r.in_c.at[chip]
            ).start()

        @pl.when(chip != there)
        def _():
            remote(
                piece(r.combc, w, rows),
                r.cbuf.at[chip],
                r.deal_c.at[w],
                r.in_c.at[chip],
                seq=2 * there + core,
            ).start()

    turns(lax.rem(chip, owners), owners, deal_back)
    adapters(r)

    def holder(q):
        return 2 * q + 1 - q // owners

    def scatter(q):
        @pl.when(jnp.logical_and(q < holders, holder(q) != me))
        def _():
            remote(
                r.red.at[pl.ds(q * share, share)],
                r.gather.at[me],
                r.red_s.at[q],
                r.red_r.at[me],
                seq=holder(q),
            ).start()

    turns(chip, chips, scatter)
    mixtures(r)

    @pl.when(holding)
    def _():
        def take(j, carry):
            arrived(r.cbuf.at[j], r.in_c.at[j])
            return carry

        lax.fori_loop(0, chips, take, 0)
        state = jnp.zeros((rows, DK), F32)
        for t in range(chips):
            j = chips - 1 - t
            r.tbuf[j] = state
            state = dot3(split(state), (r.ah[j], r.al[j])) + r.cbuf[j]
        deliver(chips, chip, core, rows, r.tbuf, r.gout, r.send_g, r.in_g)

    @pl.when(summing)
    def _():
        r.gather[me] = r.red[pl.ds(chip * share, share)]

        def got(s, carry):
            other = lax.rem(me + s, count)
            arrived(r.gather.at[other], r.red_r.at[other])
            return carry

        def add(s, total):
            return total + r.gather[s]

        lax.fori_loop(1, count, got, 0)
        r.zbuf[line] = lax.fori_loop(0, count, add, jnp.zeros((share, RANK, 128), F32))
        for peer in peers:
            remote(
                r.zbuf.at[line], r.zbuf.at[line], r.z_s.at[peer], r.z_r.at[line], head=peer
            ).start()
        for peer in peers:
            arrived(r.zbuf.at[peer], r.z_r.at[peer])
        every = r.zbuf[0]
        for z in range(1, lines):
            every = every + r.zbuf[z]
        block = chip * share + lax.broadcasted_iota(jnp.int32, (share, RANK, 128), 0)
        own = r.fin.at[pl.ds(chip * share, share)]
        own[...] = jnp.where(block < HEADS, r.zbuf[line], every)

        def tell(s, carry):
            other = lax.rem(me + s, count)
            remote(own, own, r.fin_s.at[other], r.fin_r.at[chip], seq=other).start()
            return carry

        lax.fori_loop(1, count, tell, 0)

    for w in range(owners):
        arrived(piece(r.gout, w, rows), r.in_g.at[w])
    for n in range(OWN):
        leaving = r.gout[n]
        between = dot3(split(leaving), split(r.second[n])) + r.secondc[n]
        r.ds[mine + n] = jnp.where(lead, between, leaving)
        r.stageg[n] = jnp.where(lead, leaving, between)
    for n in range(OWN):
        remote(
            r.stageg.at[n], r.ds.at[mine + n], r.fix_gs.at[n], r.fix_g.at[n], seq=sibling
        ).start()

    for n in range(OWN):
        arrived(r.siba.at[n], r.pair_as.at[n])
        arrived(r.sibb.at[n], r.pair_bs.at[n])
        arrived(r.sibc.at[n], r.pair_cs.at[n])
        arrived(r.stage.at[n], r.fix_s.at[n])

    def dealt(w):
        @pl.when(chip != core * owners + w)
        def _():
            arrived(r.abuf.at[w], r.deal_a.at[w])
            arrived(r.bbuf.at[w], r.deal_b.at[w])
            arrived(r.cbuf.at[w], r.deal_c.at[w])

    turns(lax.rem(chip, owners), owners, dealt)

    @pl.when(holding)
    def _():
        def settle(s, carry):
            other = lax.rem(chip + s, chips)
            arrived(r.sbuf.at[other], r.send.at[other])
            arrived(r.tbuf.at[other], r.send_g.at[other])
            return carry

        lax.fori_loop(1, chips, settle, 0)

    def heard(q):
        @pl.when(jnp.logical_and(q < holders, holder(q) != me))
        def _():
            arrived(r.gather.at[q], r.red_s.at[q])
            arrived(r.fin.at[pl.ds(q * share, share)], r.fin_r.at[q])

    turns(chip, chips, heard)

    @pl.when(summing)
    def _():
        for peer in peers:
            arrived(r.zbuf.at[peer], r.z_s.at[peer])

        def told(s, carry):
            other = lax.rem(me + s, count)
            arrived(r.fin.at[pl.ds(chip * share, share)], r.fin_s.at[other])
            return carry

        lax.fori_loop(1, count, told, 0)

    for n in range(OWN):
        arrived(r.stageg.at[n], r.fix_gs.at[n])
        arrived(r.ds.at[theirs + n], r.fix_g.at[n])


VM = pl.BlockSpec(memory_space=pltpu.VMEM)
SM = pl.BlockSpec(memory_space=pltpu.SMEM)
LIMIT = 56 * 1024 * 1024


def struct(*shape, dtype=F32):
    return jax.ShapeDtypeStruct(shape, dtype)


DMA = pltpu.SemaphoreType.DMA


def body(
    query_matrix_rows,
    key_matrix_rows,
    value_matrix_rows,
    write_strength,
    forget_gate_code,
    value_to_key_head,
    output_norm_gain,
    output_weight,
    adapter_lowering,
    adapter_raising,
    output_gradient,
):
    count, lines = lax.axis_size("seq"), lax.axis_size("head")
    width = output_gradient.shape[1]
    blocks = HEADS + width // 128
    chips = count // 2
    rows = OWN * DV // (chips // 2)
    share = -(-blocks // chips)
    arguments = dict(
        which=value_to_key_head,
        q=query_matrix_rows,
        k=key_matrix_rows,
        v=value_matrix_rows,
        rate=write_strength,
        code=forget_gate_code,
        gain=output_norm_gain.reshape(1, DV),
        weight=output_weight,
        lower=adapter_lowering,
        lift=adapter_raising,
        og=output_gradient,
    )
    results = dict(
        s0=(HEADS, DV, DK),
        ds=(HEADS, DV, DK),
        xt=(HEADS, DV, TOK),
        zt=(HEADS, DK, TOK),
        uf=(HEADS, TOK, DV),
        ft=(HEADS, DK, TOK),
        rows=(128, TOK),
        cols=(TOK, 128),
        fin=(blocks, RANK, 128),
        dq=(TOK, KEYS * DK),
    )

    def full(*shape):
        return pltpu.VMEM(shape, F32)

    def small(*shape):
        return pltpu.VMEM(shape, BF16)

    scratch = dict(
        k4=small(KEYS, TOK, DK),
        q4=small(KEYS, TOK, DK),
        kt4=small(KEYS, DK, TOK),
        qt4=small(KEYS, DK, TOK),
        kk4=full(KEYS, TOK, TOK),
        qk4=full(KEYS, TOK, TOK),
        gn=full(TOK, HEADS * DV),
        red=full(blocks, RANK, 128),
        grh=small(RANK, TOK),
        grl=small(RANK, TOK),
        ah=small(chips, DK, DK),
        al=small(chips, DK, DK),
        abuf=full(chips, DK, DK),
        gather=full(count, share, RANK, 128),
        zbuf=full(lines, share, RANK, 128),
    )
    scratch |= {name: small(HEADS, TOK, TOK) for name in ("th", "tl", "yh", "yl")}
    scratch |= {name: full(HEADS, TOK, DK) for name in ("w", "u", "e", "o", "do", "dqh")}
    scratch |= {name: small(HEADS, TOK, DV) for name in ("nh", "nl")}
    scratch |= {name: small(HEADS, DV, TOK) for name in ("dth", "dtl")}
    scratch |= {name: full(HEADS, DK, DV) for name in ("a", "b", "ct")}
    scratch |= {
        name: full(OWN, DK, DV)
        for name in (
            ("siba", "sibb", "sibc", "comb", "combb", "combc", "first", "second")
            + ("firstb", "secondc", "gin", "gout", "stage", "stageg")
        )
    }
    scratch |= {name: full(chips, rows, DK) for name in ("bbuf", "cbuf", "sbuf", "tbuf")}
    for number, those in (
        (OWN, ("pair_a", "pair_b", "pair_c", "pair_as", "pair_bs", "pair_cs")),
        (OWN, ("fix_s", "fix_r", "fix_gs", "fix_g")),
        (chips, ("deal_a", "deal_b", "deal_c", "in_a", "in_b", "in_c")),
        (chips, ("send", "send_g", "in_s", "in_g", "red_s", "fin_r")),
        (count, ("red_r", "fin_s")),
        (lines, ("z_s", "z_r")),
    ):
        scratch |= {name: pltpu.SemaphoreType.DMA((number,)) for name in those}
    names = (*arguments, *results, *scratch)
    found = pl.pallas_call(
        functools.partial(main_kernel, count, lines, blocks, names),
        out_shape=tuple(struct(*shape) for shape in results.values()),
        in_specs=[SM] + [VM] * (len(arguments) - 1),
        out_specs=(VM,) * len(results),
        scratch_shapes=list(scratch.values()),
        compiler_params=pltpu.CompilerParams(
            collective_id=0, has_side_effects=True, vmem_limit_bytes=LIMIT
        ),
        name="main_pass",
    )(*arguments.values())
    got = dict(zip(results, found))
    dq, dk, dv, db, grad_down, raising_gradient = pl.pallas_call(
        last_kernel,
        out_shape=(
            struct(TOK, KEYS * DK),
            struct(TOK, KEYS * DK),
            struct(TOK, HEADS * DV),
            struct(HEADS, TOK),
            struct(RANK, HEADS * DV),
            struct(RANK, width),
        ),
        in_specs=[SM] + [VM] * 11,
        out_specs=(VM,) * 6,
        scratch_shapes=[
            pltpu.VMEM((KEYS, TOK, DK), BF16),
            pltpu.VMEM((KEYS, DK, TOK), BF16),
            pltpu.VMEM((KEYS, TOK, DK), F32),
            pltpu.VMEM((KEYS, DK, TOK), F32),
        ],
        compiler_params=pltpu.CompilerParams(vmem_limit_bytes=LIMIT),
        name="last_pass",
    )(
        value_to_key_head,
        got["ds"],
        got["s0"],
        key_matrix_rows,
        *(got[name] for name in ("xt", "zt", "uf", "ft", "rows", "cols", "fin", "dq")),
    )
    return (dq, dk, dv, db, grad_down, raising_gradient)


def solution(mesh):
    placed = (
        P("seq", "head"),
        P("seq", "head"),
        P("seq", "head"),
        P("head", "seq"),
        P("head", "seq"),
        P("head"),
        P(),
        P("head", None),
        P(None, "head"),
        P(),
        P("seq", None),
    )
    return jax.shard_map(
        body,
        mesh=mesh,
        in_specs=placed,
        out_specs=(
            P("seq", "head"),
            P("seq", "head"),
            P("seq", "head"),
            P("head", "seq"),
            P(None, "head"),
            P(),
        ),
        check_vma=False,
    )
```

time: 1510 us -> 83.6 us (0.06); the launches traced: 1490 us -> 83.5 us
  other arithmetic: 847 us -> 0 us
  matrix products: 368 us -> 0 us
  waiting for transfers between devices: 151 us -> 0 us
  local copies, waits for them, and re-layouts: 91.2 us -> 0 us
  Pallas kernels: 0 us -> 82.9 us
    another operation x85 -> x0, other arithmetic: 821 us -> none  [the longest x72 819 us: block_step(): lax.linalg.triangular_solve(identity + strict_part, targets, left_side=Tr...]
    dot_general x184 -> x0, matrix products: 337 us -> none  [the longest x62 117 us: compose(): jnp.einsum('hij,hjk->hik', second_part[0], first_part[1], precision=fines...]
    all_gather x4 -> x0, waiting for transfers between devices: 150 us -> none  [prefix(): pieces = jax.tree.map(lambda part: lax.all_gather(part, axis), value)]
    pallas_call x0 -> x2, Pallas kernels: none -> 82.9 us  [the longest x1 72.1 us: body(): pl.pallas_call(functools.partial(main_kernel, count, lines, blocks, names...]
    another operation x20 -> x0, matrix products: 31.3 us -> none  [block_step(): lax.linalg.triangular_solve(identity + strict_part, targets, left_side=Tr...]
    rev x2 -> x0, local copies, waits for them, and re-layouts: 23.4 us -> none  [prefix(): pieces = jax.tree.map(lambda part: part[::-1], pieces)]
    another operation x21 -> x0, local copies, waits for them, and re-layouts: 16.1 us -> none
  transfers between devices with their start and end apart: 5 -> 0, of which waited for: 3 -> 0; matrix products, arithmetic and copies ran while one was open for 74% -> 0% of each run, Pallas kernels for 0% -> 0%
where the time goes in v3:
time: 83.6 us; the launch traced here: 83.5 us
  Pallas kernels  82.9 us (99%)
    pallas_call x1, Pallas kernels, body(): pl.pallas_call(functools.partial(main_kernel, count, lines, blocks, names...  72.1 us
    pallas_call x1, Pallas kernels, body(): pl.pallas_call(last_kernel, out_shape=(struct(TOK, KEYS * DK), struct(TOK...  10.8 us

profile of v3, /device:TPU:1, one launch (start us, length us, event | category | flops | bytes accessed | tf_op | source)
XLA Modules:
  0.0 83.5 jit_solution(4008437067432064135)
XLA Ops:
  0.6 72.1 %main_pass.1 = (f32[8,128,128]{2,1,0:T(8,128)}, f32[8,128,128]{2,1,0:T(8,128)}, f32[8,128,256]{2,1,0:T(8,128)}, f32[8,128,256]{2,1,0:T(8,128)}, f32[8,256,128]{2...) custom-call(s32[8]{0:T(128)} %which.1, ...), custom_call_target="tpu_custom_call" | custom-call | tf_op jit(solution)/shard_map/main_pass/pallas_call | solution.py:775
  72.7 10.8 %last_pass.1 = (f32[256,512]{1,0:T(8,128)}, f32[256,512]{1,0:T(8,128)}, f32[256,1024]{1,0:T(8,128)}, f32[8,256]{1,0:T(8,128)}, f32[16,1024]{1,0:T(8,128)}, /*index=5*/f32[16,2048]{1,0:T(8,128)}) custom-call(s32[8]{0:T(128)} %which.1, f32[8,128,128]{2,1,0:T(8,128)} %get-tuple-element.16.ds_ref, f32[8,128,128]{2,1,0:T(8,128)} %get-tuple-element.17.s0_ref, ...), custom_call_target="tpu_custom_call" | custom-call | tf_op jit(solution)/shard_map/last_pass/pallas_call | solution.py:787
